TPU v7x, 256 devices: a whole 4x4x8 slice. The times are simulated.
256 devices in a mesh: dp: 32 (over y, x, core), proto: 8 (over z).
Axes of the slice: x: 4, y: 4, z: 8, core: 2. Of those that a mesh axis runs over, the one named last changes fastest.
Arguments:
- teacher_patches: bfloat16 [24576, 256], P('dp'), may hold values from -8 to 8
- student_patches: bfloat16 [24576, 256], P('dp'), may hold values from -6 to 6
- mask_index: int32 [12288], P('dp'), may hold values from 0 to 767
- teacher_weight: bfloat16 [256, 65536], P(None, 'proto'), may hold values from -8 to 8
- student_weight: bfloat16 [256, 65536], P(None, 'proto'), may hold values from -0.375 to 0.375
Outputs:
- loss: float32 [12288], P('dp')
- grad_weight: float32 [256, 65536], P('dp', 'proto')
- grad_patches: float32 [24576, 256], P('dp')
Inputs may be any that keep to these rules, and one draw needn't show every extreme that they name: `mask_index`: entries may repeat within a block of 384 rows.
All inputs are finite; a program needn't handle non-finite values.
Results may differ from a plain program's by a relative error of at most 0.001.
The roundings to bfloat16 on the way count: a program that leaves them out, or rounds other values in their place, can miss the bound.
Values sent between devices are 32-bit elements; how exact they have to be, the bound alone decides.
A program may use at most 128 MiB of HBM per device.

v0:
```python
import jax
import jax.numpy as jnp
from jax import lax
from jax.sharding import PartitionSpec as P

ITERS = 3


epsilon = 1e-06
TEACHER_TEMP = 0.07
STUDENT_TEMP = 0.1


def normalized_rows(values):
    wide = values.astype(jnp.float32)
    inverse = lax.rsqrt(jnp.sum(wide * wide, axis=1, keepdims=True) + epsilon)
    return ((wide * inverse).astype(jnp.bfloat16), inverse, wide)


def normalized_columns(values):
    wide = values.astype(jnp.float32)
    inverse = lax.rsqrt(jnp.sum(wide * wide, axis=0, keepdims=True) + epsilon)
    return ((wide * inverse).astype(jnp.bfloat16), inverse, wide)


def shards(teacher_patches, student_patches, mask_index, teacher_weight, student_weight):
    dp_count = lax.axis_size("dp")
    rows_here = mask_index.shape[0]
    width = teacher_weight.shape[0]
    proto_here = teacher_weight.shape[1]
    rows_total = rows_here * dp_count
    proto_total = proto_here * lax.axis_size("proto")
    teacher_rows = jnp.take(teacher_patches, mask_index, axis=0)
    student_rows = jnp.take(student_patches, mask_index, axis=0)
    teacher_unit = normalized_rows(teacher_rows)[0]
    student_unit, row_inverse, student_wide = normalized_rows(student_rows)
    teacher_proto = normalized_columns(teacher_weight)[0]
    student_proto, column_inverse, weight_wide = normalized_columns(student_weight)
    teacher_exp = jnp.exp(
        jnp.dot(teacher_unit, teacher_proto, preferred_element_type=jnp.float32) / TEACHER_TEMP
    )
    logits = jnp.dot(student_unit, student_proto, preferred_element_type=jnp.float32) / STUDENT_TEMP
    student_exp = jnp.exp(logits)
    student_part = jnp.sum(student_exp, axis=1)
    student_total = lax.psum(student_part, "proto")
    row_scale = jnp.ones((rows_here,), jnp.float32)
    col_scale = jnp.ones((proto_here,), jnp.float32)
    for sweep in range(ITERS):
        col_part = jnp.dot(row_scale, teacher_exp, precision=lax.Precision.HIGHEST)
        col_sum = col_scale * lax.psum(col_part, "dp")
        col_scale = col_scale / (col_sum * proto_total)
        row_part = jnp.dot(teacher_exp, col_scale, precision=lax.Precision.HIGHEST)
        if sweep == 0:
            row_total = lax.psum(row_part, "proto")
        else:
            row_total = lax.psum(row_part, "proto")
        row_sum = row_scale * row_total
        row_scale = row_scale / (row_sum * rows_total)
    targets = (rows_total * row_scale)[:, None] * teacher_exp * col_scale[None, :]
    log_total = jnp.log(student_total)
    loss_part = jnp.sum(targets * (logits - log_total[:, None]), axis=1)
    loss = -lax.psum(loss_part, "proto")
    probs = student_exp / student_total[:, None]
    grad_logits = ((probs - targets) / (rows_total * STUDENT_TEMP)).astype(jnp.bfloat16)
    feature_part = lax.dot_general(
        grad_logits, student_proto, (((1,), (1,)), ((), ())), preferred_element_type=jnp.float32
    )
    feature_grad = lax.psum(feature_part, "proto")
    row_grad = row_inverse * feature_grad - student_wide * row_inverse**3 * jnp.sum(
        student_wide * feature_grad, axis=1, keepdims=True
    )
    patch_ids = jnp.arange(teacher_patches.shape[0], dtype=jnp.int32)
    one_hot = (patch_ids[:, None] == mask_index[None, :]).astype(jnp.float32)
    grad_patches = jnp.dot(one_hot, row_grad, precision=lax.Precision.HIGHEST)
    bot_here = width // dp_count
    proto_grad = lax.psum_scatter(
        lax.dot_general(
            student_unit, grad_logits, (((0,), (0,)), ((), ())), preferred_element_type=jnp.float32
        ),
        "dp",
        scatter_dimension=0,
        tiled=True,
    )
    own_rows = lax.dynamic_slice_in_dim(weight_wide, lax.axis_index("dp") * bot_here, bot_here, 0)
    inner = lax.psum(jnp.sum(own_rows * proto_grad, axis=0), "dp")
    grad_weight = column_inverse * proto_grad - own_rows * column_inverse**3 * inner[None, :]
    return (loss, grad_weight, grad_patches)


def solution(mesh):
    placed = (P("dp", None), P("dp", None), P("dp"), P(None, "proto"), P(None, "proto"))
    return jax.shard_map(
        shards,
        mesh=mesh,
        in_specs=placed,
        out_specs=(P("dp"), P("dp", "proto"), P("dp", None)),
        check_vma=False,
    )
```

profile of v0, /device:TPU:1, one launch (start us, length us, event | category | flops | bytes accessed | tf_op | source)
XLA Modules:
  0.0 773.5 jit_solution(5842610871085047194)
XLA Ops:
  9.5 2.1 gather_fusion.1
  11.6 2.7 gather_fusion
  14.3 3.1 fusion
  17.7 4.8 multiply_exponential_fusion
  22.5 4.5 copy-done.1
  27.0 6.0 fusion.24
  33.0 124.7 %psum.70 = f32[8192]{0:T(1024)S(1)} all-reduce(f32[8192]{0:T(1024)S(1)} %bitcast.23), channel_id=1, replica_groups=mesh['dp'=32,'proto'=8] {'dp'}, use_global_device_ids=true, to_apply=%region_2.4 | all-reduce | flops 8192 | bytes 65536 | tf_op jit(solution)/shard_map/psum | solution.py:50
  157.7 13.3 %convolution_reduce_fusion.2 = f32[384]{0:T(512)S(1)} fusion(f32[384,8192]{1,0:T(8,128)} %copy-done.1, f32[8192,1]{0,1:T(1,128)S(1)} %bitcast.24), kind=kOutput, calls=%fused_computation.20 | convolution fusion | flops 37748736 | bytes 12617216 | tf_op jit(solution)/shard_map/dot_general | solution.py:52
  170.9 16.2 %psum.71 = f32[384]{0:T(512)S(1)} all-reduce(f32[384]{0:T(512)S(1)} %convolution_reduce_fusion.2), channel_id=1, replica_groups=mesh['dp'=32,'proto'=8] {'proto'}, use_global_device_ids=true, to_apply=%region_3.5 | all-reduce | flops 384 | bytes 3072 | tf_op jit(solution)/shard_map/psum | solution.py:54
  187.2 8.9 %fusion.28 = f32[1,8192]{1,0:T(1,128)S(1)} fusion(f32[384,1]{0,1:T(1,128)S(1)} %reshape.80, f32[384,8192]{1,0:T(8,128)} %copy-done.1), kind=kOutput, calls=%fused_computation.66 | convolution fusion | flops 37748736 | bytes 12617216 | tf_op jit(solution)/shard_map/dot_general | solution.py:49
  196.1 127.5 %psum.72 = f32[8192]{0:T(1024)S(1)} all-reduce(f32[8192]{0:T(1024)S(1)} %bitcast.21), channel_id=1, replica_groups=mesh['dp'=32,'proto'=8] {'dp'}, use_global_device_ids=true, to_apply=%region_4.6 | all-reduce | flops 8192 | bytes 65536 | tf_op jit(solution)/shard_map/psum | solution.py:50
  323.6 13.3 %convolution_reduce_fusion.1 = f32[384]{0:T(512)S(1)} fusion(f32[384,8192]{1,0:T(8,128)} %copy-done.1, f32[8192,1]{0,1:T(1,128)S(1)} %bitcast.20), kind=kOutput, calls=%fused_computation.19 | convolution fusion | flops 37748736 | bytes 12617216 | tf_op jit(solution)/shard_map/dot_general | solution.py:52
  336.9 10.9 %psum.73 = f32[384]{0:T(512)S(1)} all-reduce(f32[384]{0:T(512)S(1)} %convolution_reduce_fusion.1), channel_id=1, replica_groups=mesh['dp'=32,'proto'=8] {'proto'}, use_global_device_ids=true, to_apply=%region_5.7 | all-reduce | flops 384 | bytes 3072 | tf_op jit(solution)/shard_map/psum | solution.py:56
  347.8 8.9 %fusion.29 = f32[1,8192]{1,0:T(1,128)S(1)} fusion(f32[384,1]{0,1:T(1,128)S(1)} %reshape.84, f32[384,8192]{1,0:T(8,128)} %copy-done.1), kind=kOutput, calls=%fused_computation.67 | convolution fusion | flops 37748736 | bytes 12617216 | tf_op jit(solution)/shard_map/dot_general | solution.py:49
  356.7 127.2 %psum.74 = f32[8192]{0:T(1024)S(1)} all-reduce(f32[8192]{0:T(1024)S(1)} %bitcast.22), channel_id=1, replica_groups=mesh['dp'=32,'proto'=8] {'dp'}, use_global_device_ids=true, to_apply=%region_6.8 | all-reduce | flops 8192 | bytes 65536 | tf_op jit(solution)/shard_map/psum | solution.py:50
  483.9 13.4 %convolution_reduce_fusion = f32[384]{0:T(512)S(1)} fusion(f32[384,8192]{1,0:T(8,128)} %copy-done.1, f32[8192,1]{0,1:T(1,128)S(1)} %bitcast.19), kind=kOutput, calls=%fused_computation.18 | convolution fusion | flops 37748736 | bytes 12617216 | tf_op jit(solution)/shard_map/dot_general | solution.py:52
  497.4 0.9 multiply_reduce_fusion.1
  498.3 6.0 exponential_reduce_fusion
  504.3 12.6 %all-reduce = (f32[384]{0:T(512)S(1)}, f32[384]{0:T(512)S(1)}) all-reduce(f32[384]{0:T(512)S(1)} %get-tuple-element.14, f32[384]{0:T(512)S(1)} %convolution_reduce_fusion), channel_id=1, replica_groups=mesh['dp'=32,'proto'=8] {'proto'}, use_global_device_ids=true, to_apply=%region_11.13 | all-reduce | flops 768 | bytes 6144 | tf_op jit(solution)/shard_map/psum | solution.py:45
  516.9 10.8 %multiply_convert_fusion = (bf16[384,8192]{1,0:T(8,128)(2,1)S(1)}, f32[384]{0:T(512)S(1)}) fusion(f32[384,8192]{1,0:T(8,128)} %get-tuple-element.15, f32[384,8192]{1,0:T(8,128)} %copy-done.1, f32[384]{0:T(512)S(1)} %get-tuple-element.6, f32[8192]{0:T(1024)S(1)} %multiply_divide_fusion, f32[384]{0:T(512)S(1)} %divide_multiply_fusion, f32[384]{0:T(512)S(1)} %log.3), kind=kLoop, calls=%fused_computation.2 | loop fusion | flops 28311168 | bytes 31496192 | tf_op jit(solution)/shard_map/convert_element_type | solution.py:64
  527.7 2.7 copy-done.4
  530.4 2.6 fusion.4
  533.1 8.5 %fusion.21 = f32[256,8192]{1,0:T(8,128)} fusion(bf16[384,8192]{1,0:T(8,128)(2,1)} %copy-done.4, f32[384]{0:T(512)S(1)} %get-tuple-element.13, bf16[384,256]{1,0:T(8,128)(2,1)S(1)} %gather_fusion.1, pred[384]{0:T(512)(128)(4,1)S(1)} %compare_and_fusion), kind=kOutput, calls=%fused_computation.44 | convolution fusion | flops 1611005952 | bytes 14878592 | tf_op jit(solution)/shard_map/dot_general | solution.py:77
  541.6 6.4 convert_element_type.34
  548.0 10.9 %psum.77 = f32[384]{0:T(512)S(1)} all-reduce(f32[384]{0:T(512)S(1)} %get-tuple-element.9), channel_id=1, replica_groups=mesh['dp'=32,'proto'=8] {'proto'}, use_global_device_ids=true, to_apply=%region_13.15 | all-reduce | flops 384 | bytes 3072 | tf_op jit(solution)/shard_map/psum | solution.py:62
  559.5 44.0 %all-reduce.3.cloned.1.call-done = f32[384,256]{1,0:T(8,128)} async-done(((f32[384,256]{1,0:T(8,128)}), f32[384,256]{1,0:T(8,128)}) %all-reduce.3.cloned.1.call-update) | async-done | bytes 393232 | tf_op jit(solution)/shard_map/psum | solution.py:68
  603.6 1.2 fusion.14
  604.8 2.9 fusion.5
  607.7 34.4 %reduce-scatter.2.cloned.1.call-done = f32[8,8192]{1,0:T(8,128)} async-done(((f32[256,8192]{1,0:T(8,128)}), f32[8,8192]{1,0:T(8,128)}) %reduce-scatter.2.cloned.1.call-update) | async-done | bytes 262160 | tf_op jit(solution)/shard_map/reduce_scatter | solution.py:76
  642.1 1.1 multiply_reduce_fusion.2
  643.2 120.9 %psum.78 = f32[8192]{0:T(1024)S(1)} all-reduce(f32[8192]{0:T(1024)S(1)} %multiply_reduce_fusion.2), channel_id=1, replica_groups=mesh['dp'=32,'proto'=8] {'dp'}, use_global_device_ids=true, to_apply=%region_16.18 | all-reduce | flops 8192 | bytes 65536 | tf_op jit(solution)/shard_map/psum | solution.py:85
  764.1 1.8 multiply_subtract_fusion
  (31 shorter events, 2.6 us)
Async XLA Ops:
  8.0 1.5 copy-start
  8.0 595.6 %all-reduce.3.cloned.1.call-start = ((), (), s32[]{:S(2)}) async-start(), calls=%async_computation.2 | async-start | bytes 786432 | tf_op jit(solution)/shard_map/psum | solution.py:68
  22.5 4.5 copy-start.1
  483.9 13.4 %copy-start.2 = (bf16[256,8192]{1,0:T(8,128)(2,1)S(1)}, bf16[256,8192]{1,0:T(8,128)(2,1)}, u32[]{:S(2)}) copy-start(bf16[256,8192]{1,0:T(8,128)(2,1)} %param.11) | copy-start | bytes 12582916
  516.9 13.5 %copy-start.3 = (bf16[256,8192]{1,0:T(8,128)(2,1)S(1)}, bf16[256,8192]{1,0:T(8,128)(2,1)}, u32[]{:S(2)}) copy-start(bf16[256,8192]{1,0:T(8,128)(2,1)} %param.11) | copy-start | bytes 12582916
  527.7 2.7 copy-start.4
  533.0 109.0 %reduce-scatter.2.cloned.1.call-start = ((), (), s32[]{:S(2)}) async-start(), calls=%async_computation.1 | async-start | bytes 8650752 | tf_op jit(solution)/shard_map/reduce_scatter | solution.py:76
  541.6 63.2 %copy-start.5 = (s32[384]{0:T(512)S(1)}, s32[384]{0:T(512)}, u32[]{:S(2)}) copy-start(s32[384]{0:T(512)} %param.9) | copy-start | bytes 4612
Sparse Core Ops, SparseCore 0:
  533.2 70.3 all-reduce.2
Sparse Core Ops, SparseCore 1:
  541.7 100.3 reduce-scatter.1
where the time goes:
time: 786 us; the launch traced here: 774 us
  blocking collectives  551 us (70%)
  matrix products  88.5 us (11%)
  waiting for transfers between devices  78.4 us (10%)
  other arithmetic  27.6 us (4%)
  between operations  15.9 us (2%)
  local copies, waits for them, and re-layouts  12 us (2%)
    psum x3, blocking collectives, shards(): col_sum = col_scale * lax.psum(col_part, 'dp')  379 us
    psum x1, blocking collectives, shards(): inner = lax.psum(jnp.sum(own_rows * proto_grad, axis=0), 'dp')  121 us
    psum x1, waiting for transfers between devices, shards(): feature_grad = lax.psum(feature_part, 'proto')  44 us
    dot_general x3, matrix products, shards(): row_part = jnp.dot(teacher_exp, col_scale, precision=lax.Precision.HIGHEST)  39.9 us
    reduce_scatter x1, waiting for transfers between devices, shards(): lax.psum_scatter(lax.dot_general(student_unit, grad_logits, (((0,), (0,))...  34.4 us
    psum x2, blocking collectives, shards(): row_total = lax.psum(row_part, 'proto')  27.1 us
    dot_general x3, matrix products, shards(): col_part = jnp.dot(row_scale, teacher_exp, precision=lax.Precision.HIGHEST)  23.8 us
  transfers between devices with their start and end apart: 2, of which 2 were waited for; matrix products, arithmetic and copies ran while one was open for 3% of the time, Pallas kernels for 0%

commit v1 on v0

v1 whole, which is shorter than its diff:
```python
import functools
import math

import jax
import jax.numpy as jnp
from jax import lax
from jax.experimental import pallas as pl
from jax.experimental.pallas import tpu as pltpu
from jax.sharding import PartitionSpec as P

MESH = pl.DeviceIdType.MESH
F32 = jnp.float32
BF16 = jnp.bfloat16

EPS = 1e-06
TEACHER_TEMP = 0.07
STUDENT_TEMP = 0.1
LOG2E = 1.0 / math.log(2.0)

NY, NX, NK, NZ = 4, 4, 2, 8
DP = NY * NX * NK
CHIPS = NY * NX
OWN = 384
ROWS = NK * OWN
WIDTH = 256
PATCH = 768
COLS = 4096
LANES = 128
CH = 512
PARTS = COLS // CH
BLOCK = 256
TOTAL_ROWS = OWN * DP
TOTAL_PROTOS = COLS * NK * NZ
ZROWS = OWN // NZ
GRAD_SCALE = 1.0 / (TOTAL_ROWS * STUDENT_TEMP)
COL_PEERS = [(dy, dx) for dy in range(NY) for dx in range(NX)]
ROW_PEERS = [(dz, dk) for dz in range(NZ) for dk in range(NK)]


def aligned(value, unit):
    return pl.multiple_of(value, unit)


def kernel(
    tpat, spat, midx, tw_hbm, sw_hbm,
    loss_ref, gw_ref, gp_ref,
    tw, sw, tp, sp, cinv, units, tu, su, sut, onehot_t, srow, rinv,
    e_ref, l_ref, part, part2, csend, crecv, cscale, rsend, rrecv, rcol, ltot,
    grad, pg, r1, r2, r3, r4, second, feat, fsib, fz, rg, gwfull, lossrow,
    load_sem, unit_send, unit_recv, col_send, col_recv, row_send, row_recv,
    rs_send, rs_recv, feat_send, feat_recv, gw_send, gw_recv,
):
    dp = lax.axis_index("dp")
    z = lax.axis_index("proto")
    k = lax.rem(dp, NK)
    chip = lax.div(dp, NK)
    x = lax.rem(chip, NX)
    y = lax.div(chip, NX)

    def device(yy, xx, kk, zz):
        return ((yy * NX + xx) * NK + kk, zz)

    def chip_at(dy, dx):
        return device(lax.rem(y + dy, NY), lax.rem(x + dx, NX), k, z)

    def row_at(dz, dk):
        return device(y, x, lax.rem(k + dk, NK), lax.rem(z + dz, NZ))

    sibling = row_at(0, 1)

    def send(src, dst, send_sem, recv_sem, where):
        copy = pltpu.make_async_remote_copy(
            src_ref=src, dst_ref=dst, send_sem=send_sem, recv_sem=recv_sem,
            device_id=where, device_id_type=MESH,
        )
        copy.start()

    def await_bytes(ref, sem):
        pltpu.make_async_copy(ref, ref, sem).wait()

    barrier = pltpu.get_barrier_semaphore()
    for dy, dx in COL_PEERS[1:]:
        pl.semaphore_signal(barrier, inc=1, device_id=chip_at(dy, dx), device_id_type=MESH)
    for dz, dk in ROW_PEERS[1:]:
        pl.semaphore_signal(barrier, inc=1, device_id=row_at(dz, dk), device_id_type=MESH)

    mine = pl.ds(aligned(k * COLS, COLS), COLS)
    load_t = pltpu.make_async_copy(tw_hbm.at[:, mine], tw, load_sem.at[0])
    load_s = pltpu.make_async_copy(sw_hbm.at[:, mine], sw, load_sem.at[1])
    load_t.start()
    load_s.start()

    index = midx[...].reshape(1, OWN)
    index_col = jnp.transpose(jnp.broadcast_to(index.astype(F32), (LANES, OWN)))
    lane = lax.broadcasted_iota(jnp.int32, (OWN, LANES), 1).astype(F32)
    onehot = jnp.concatenate(
        [jnp.where(index_col == lane + float(t * LANES), 1.0, 0.0) for t in range(PATCH // LANES)], axis=1
    ).astype(BF16)
    patch_id = lax.broadcasted_iota(jnp.int32, (PATCH, OWN), 0)
    onehot_t[...] = jnp.where(patch_id == index, 1.0, 0.0).astype(BF16)
    trow = jnp.dot(onehot, tpat[...], preferred_element_type=F32)
    srow_value = jnp.dot(onehot, spat[...], preferred_element_type=F32)
    tinv = lax.rsqrt(jnp.sum(trow * trow, axis=1, keepdims=True) + EPS)
    sinv = lax.rsqrt(jnp.sum(srow_value * srow_value, axis=1, keepdims=True) + EPS)
    srow[...] = srow_value
    rinv[...] = jnp.broadcast_to(sinv, (OWN, LANES))
    units[0, k] = (trow * tinv).astype(BF16).astype(F32)
    units[1, k] = (srow_value * sinv).astype(BF16).astype(F32)

    pl.semaphore_wait(barrier, CHIPS - 1 + NZ * NK - 1)
    for side in range(2):
        send(units.at[side, k], units.at[side, k], unit_send.at[side], unit_recv.at[side], sibling)

    load_t.wait()

    def teacher_columns(j, carry):
        cols = pl.ds(aligned(j * CH, CH), CH)
        wide = tw[:, cols].astype(F32)
        inverse = lax.rsqrt(jnp.sum(wide * wide, axis=0, keepdims=True) + EPS)
        tp[:, cols] = (wide * inverse).astype(BF16)
        return carry

    lax.fori_loop(0, PARTS, teacher_columns, 0)
    load_s.wait()

    def student_columns(j, carry):
        cols = pl.ds(aligned(j * CH, CH), CH)
        wide = sw[:, cols].astype(F32)
        inverse = lax.rsqrt(jnp.sum(wide * wide, axis=0, keepdims=True) + EPS)
        cinv[:, cols] = inverse
        sp[:, cols] = (wide * inverse).astype(BF16)
        return carry

    lax.fori_loop(0, PARTS, student_columns, 0)

    other = lax.rem(k + 1, NK)
    for side in range(2):
        await_bytes(units.at[side, other], unit_recv.at[side])
    for core in range(NK):
        tu[core * OWN:(core + 1) * OWN, :] = units[0, core].astype(BF16)
        su[core * OWN:(core + 1) * OWN, :] = units[1, core].astype(BF16)
        sut[1, :, core * OWN:(core + 1) * OWN] = jnp.transpose(units[1, core]).astype(BF16)
    for xx in range(NX):
        for yy in range(NY):
            to, at = (xx * NY + yy) * 16, (yy * NX + xx) * 16
            sut[0, to:to + 16, :] = sut[1, at:at + 16, :]

    def columns_start(turn):
        for slot, (dy, dx) in enumerate(COL_PEERS):
            if slot:
                send(csend.at[turn], crecv.at[turn, slot], col_send.at[turn], col_recv.at[turn], chip_at(dy, dx))

    def columns_end(turn):
        rest = crecv.at[turn, pl.ds(1, CHIPS - 1)]
        await_bytes(rest, col_recv.at[turn])
        total = csend[turn]
        for slot in range(1, CHIPS):
            total = total + crecv[turn, slot]
        return total

    def rows_start(turn, width):
        cut = pl.ds(0, width)
        for slot, (dz, dk) in enumerate(ROW_PEERS):
            if slot:
                send(
                    rsend.at[turn, :, cut], rrecv.at[turn, slot, :, cut],
                    row_send.at[turn], row_recv.at[turn], row_at(dz, dk),
                )

    def rows_end(turn, width):
        cut = pl.ds(0, width)
        await_bytes(rrecv.at[turn, pl.ds(1, NZ * NK - 1), :, cut], row_recv.at[turn])
        total = rsend[turn, :, 0:width]
        for slot in range(1, NZ * NK):
            total = total + rrecv[turn, slot, :, 0:width]
        return total

    def to_column(row):
        return jnp.transpose(jnp.broadcast_to(row, (LANES, ROWS)))

    def lane_sums(ref):
        return jnp.sum(jnp.transpose(ref[...]), axis=0, keepdims=True)

    def teacher_exp(j, carry):
        cols = pl.ds(aligned(j * CH, CH), CH)
        total = jnp.zeros((1, CH), F32)
        for rb in range(ROWS // BLOCK):
            at = slice(rb * BLOCK, (rb + 1) * BLOCK)
            value = jnp.exp2(
                jnp.dot(tu[at, :], tp[:, cols], preferred_element_type=F32) * (LOG2E / TEACHER_TEMP)
            )
            e_ref[at, cols] = value
            total = total + jnp.sum(value, axis=0, keepdims=True)
        csend[0, :, cols] = total
        return carry

    lax.fori_loop(0, PARTS, teacher_exp, 0)
    columns_start(0)

    part2[...] = jnp.zeros_like(part2)

    def student_logits(j, carry):
        cols = pl.ds(aligned(j * CH, CH), CH)
        for rb in range(ROWS // BLOCK):
            at = slice(rb * BLOCK, (rb + 1) * BLOCK)
            value = jnp.dot(su[at, :], sp[:, cols], preferred_element_type=F32) * (LOG2E / STUDENT_TEMP)
            l_ref[at, cols] = value
            power = jnp.exp2(value)
            total = part2[at, :]
            for t in range(CH // LANES):
                total = total + power[:, t * LANES:(t + 1) * LANES]
            part2[at, :] = total
        return carry

    lax.fori_loop(0, PARTS, student_logits, 0)

    STEP = 64

    def row_pass(with_loss):
        def body(rb, carry):
            at = pl.ds(aligned(rb * STEP, STEP), STEP)
            total = jnp.zeros((STEP, LANES), F32)
            cross = jnp.zeros((STEP, LANES), F32)
            for t in range(COLS // LANES):
                cut = slice(t * LANES, (t + 1) * LANES)
                value = e_ref[at, cut] * cscale[:, cut]
                total = total + value
                if with_loss:
                    cross = cross + value * l_ref[at, cut]
            part[at, :] = total
            if with_loss:
                part2[at, :] = cross
            return carry

        lax.fori_loop(0, ROWS // STEP, body, 0)

    WIDE = 1024

    def col_pass(turn):
        def body(j, carry):
            def inner(rb, totals):
                at = pl.ds(aligned(rb * STEP, STEP), STEP)
                scale = rcol[at, :]
                out = []
                for t in range(WIDE // LANES):
                    value = e_ref[at, pl.ds(aligned(j * WIDE + t * LANES, LANES), LANES)] * scale
                    out.append(totals[t] + jnp.sum(value.reshape(STEP // 8, 8, LANES), axis=0))
                return tuple(out)

            start = tuple(jnp.zeros((8, LANES), F32) for _ in range(WIDE // LANES))
            totals = lax.fori_loop(0, ROWS // STEP, inner, start)
            for t in range(WIDE // LANES):
                csend[turn, :, pl.ds(aligned(j * WIDE + t * LANES, LANES), LANES)] = jnp.sum(
                    totals[t], axis=0, keepdims=True
                )
            return carry

        lax.fori_loop(0, COLS // WIDE, body, 0)

    cscale[...] = 1.0 / (columns_end(0) * TOTAL_PROTOS)
    rsend[0, :, ROWS:2 * ROWS] = lane_sums(part2)
    row_pass(False)
    rsend[0, :, 0:ROWS] = lane_sums(part)
    rows_start(0, 2 * ROWS)
    both = rows_end(0, 2 * ROWS)
    rcol[...] = to_column(1.0 / (both[:, 0:ROWS] * TOTAL_ROWS))
    col_pass(1)
    columns_start(1)
    log_total = jnp.log(both[:, ROWS:2 * ROWS])
    ltot[...] = to_column((log_total - math.log(GRAD_SCALE)) * LOG2E)
    cscale[...] = 1.0 / (columns_end(1) * TOTAL_PROTOS)
    row_pass(False)
    rsend[1, :, 0:ROWS] = lane_sums(part)
    rows_start(1, ROWS)
    rcol[...] = to_column(1.0 / (rows_end(1, ROWS) * TOTAL_ROWS))
    col_pass(2)
    columns_start(2)
    cscale[...] = 1.0 / (columns_end(2) * TOTAL_PROTOS)
    row_pass(True)
    rsend[2, :, 0:ROWS] = lane_sums(part)
    rsend[2, :, ROWS:2 * ROWS] = lane_sums(part2)
    rows_start(2, 2 * ROWS)
    both = rows_end(2, 2 * ROWS)
    row_sum = both[:, 0:ROWS]
    row_scale = 1.0 / (row_sum * TOTAL_ROWS)
    rcol[...] = to_column(row_scale * (TOTAL_ROWS * GRAD_SCALE))
    target_sum = row_sum * (row_scale * TOTAL_ROWS)
    target_logits = both[:, ROWS:2 * ROWS] * (row_scale * (TOTAL_ROWS / LOG2E))
    lossrow[...] = log_total * target_sum - target_logits

    ahead = {0: (chip_at(0, 1), chip_at(0, 3), x), 1: (chip_at(1, 0), chip_at(3, 0), y)}
    feat[...] = jnp.zeros_like(feat)

    def gradient(j, carry):
        for kind in range(2):
            q = 2 * j + kind
            cols = pl.ds(aligned(q * CH, CH), CH)
            for rb in range(ROWS // BLOCK):
                at = slice(rb * BLOCK, (rb + 1) * BLOCK)
                scale = rcol[at, :]
                shift = ltot[at, :]
                for t in range(CH // LANES):
                    cut = pl.ds(aligned(q * CH + t * LANES, LANES), LANES)
                    probs = jnp.exp2(l_ref[at, cut] - shift)
                    target = e_ref[at, cut] * cscale[:, cut] * scale
                    grad[at, t * LANES:(t + 1) * LANES] = (probs - target).astype(BF16)
            pg[q] = jnp.dot(sut[kind], grad[...], preferred_element_type=F32)
            plus, minus, a = ahead[kind]
            opposite = lax.rem(a + 2, 4) * 64
            ap, am = lax.rem(a + 1, 4) * 64, lax.rem(a + 3, 4) * 64
            send(pg.at[q, pl.ds(aligned(opposite, 32), 32)], r1.at[q, 0], rs_send.at[q, 0], rs_recv.at[q, 0], plus)
            send(pg.at[q, pl.ds(aligned(opposite + 32, 32), 32)], r1.at[q, 1], rs_send.at[q, 0], rs_recv.at[q, 1], minus)
            send(pg.at[q, pl.ds(aligned(ap + 32, 32), 32)], r2.at[q, 0, pl.ds(32, 32)], rs_send.at[q, 0], rs_recv.at[q, 2], plus)
            send(pg.at[q, pl.ds(aligned(am, 32), 32)], r2.at[q, 1, pl.ds(0, 32)], rs_send.at[q, 0], rs_recv.at[q, 2], minus)
            inner = jnp.zeros((1, CH), F32)
            for yy in range(NY):
                for xx in range(NX):
                    at = (yy * NX + xx) * 16
                    to = (xx * NY + yy) * 16 if kind == 0 else at
                    inner = inner + jnp.sum(
                        sw[at:at + 16, cols].astype(F32) * pg[q, to:to + 16, :], axis=0, keepdims=True
                    )
            csend[3, :, cols] = inner
            feat[...] += lax.dot_general(
                grad[...], sp[:, cols], (((1,), (1,)), ((), ())), preferred_element_type=F32
            )
        return carry

    lax.fori_loop(0, PARTS // 2, gradient, 0)
    send(feat.at[pl.ds(aligned(other * OWN, OWN), OWN)], fsib, feat_send.at[0], feat_recv.at[0], sibling)
    columns_start(3)

    def first_forward(j, carry):
        for kind in range(2):
            q = 2 * j + kind
            plus, minus, a = ahead[kind]
            ap = aligned(lax.rem(a + 1, 4) * 64, 32)
            am = aligned(lax.rem(a + 3, 4) * 64 + 32, 32)
            await_bytes(r1.at[q, 0], rs_recv.at[q, 0])
            pg[q, pl.ds(ap, 32), :] = pg[q, pl.ds(ap, 32), :] + r1[q, 0]
            send(pg.at[q, pl.ds(ap, 32)], r2.at[q, 0, pl.ds(0, 32)], rs_send.at[q, 0], rs_recv.at[q, 2], plus)
            await_bytes(r1.at[q, 1], rs_recv.at[q, 1])
            pg[q, pl.ds(am, 32), :] = pg[q, pl.ds(am, 32), :] + r1[q, 1]
            send(pg.at[q, pl.ds(am, 32)], r2.at[q, 1, pl.ds(32, 32)], rs_send.at[q, 0], rs_recv.at[q, 2], minus)
        return carry

    lax.fori_loop(0, PARTS // 2, first_forward, 0)

    own_rows = pl.ds(aligned(k * OWN, OWN), OWN)
    await_bytes(fsib, feat_recv.at[0])
    feat[own_rows, :] = feat[own_rows, :] + fsib[...]
    for dz in range(1, NZ):
        to = lax.rem(z + dz, NZ)
        rows = pl.ds(aligned(k * OWN + to * ZROWS, ZROWS), ZROWS)
        send(feat.at[rows], fz.at[dz], feat_send.at[1], feat_recv.at[1], row_at(dz, 0))

    def second_start(j, carry):
        for kind in range(2):
            q = 2 * j + kind
            a = ahead[kind][2]
            plus, minus, b = ahead[1 - kind]
            await_bytes(r2.at[q], rs_recv.at[q, 2])
            second[q] = pg[q, pl.ds(aligned(a * 64, 64), 64), :] + r2[q, 0] + r2[q, 1]
            opposite = lax.rem(b + 2, 4) * 16
            bp, bm = lax.rem(b + 1, 4) * 16, lax.rem(b + 3, 4) * 16
            send(second.at[q, pl.ds(aligned(opposite, 8), 8)], r3.at[q, 0], rs_send.at[q, 1], rs_recv.at[q, 3], plus)
            send(second.at[q, pl.ds(aligned(opposite + 8, 8), 8)], r3.at[q, 1], rs_send.at[q, 1], rs_recv.at[q, 4], minus)
            send(second.at[q, pl.ds(aligned(bp + 8, 8), 8)], r4.at[q, 0, pl.ds(8, 8)], rs_send.at[q, 1], rs_recv.at[q, 5], plus)
            send(second.at[q, pl.ds(aligned(bm, 8), 8)], r4.at[q, 1, pl.ds(0, 8)], rs_send.at[q, 1], rs_recv.at[q, 5], minus)
        return carry

    lax.fori_loop(0, PARTS // 2, second_start, 0)

    await_bytes(fz.at[pl.ds(1, NZ - 1)], feat_recv.at[1])
    feature = feat[pl.ds(aligned(k * OWN + z * ZROWS, ZROWS), ZROWS), :]
    for dz in range(1, NZ):
        feature = feature + fz[dz]
    share = pl.ds(aligned(z * ZROWS, ZROWS), ZROWS)
    rows_wide = srow[share, :]
    inverse = rinv[share, 0:1]
    rg[share, :] = inverse * feature - rows_wide * (inverse * inverse * inverse) * jnp.sum(
        rows_wide * feature, axis=1, keepdims=True
    )
    for dz in range(1, NZ):
        send(rg.at[share], rg.at[share], feat_send.at[2], feat_recv.at[2], row_at(dz, 0))

    def second_forward(j, carry):
        for kind in range(2):
            q = 2 * j + kind
            plus, minus, b = ahead[1 - kind]
            bp = aligned(lax.rem(b + 1, 4) * 16, 8)
            bm = aligned(lax.rem(b + 3, 4) * 16 + 8, 8)
            await_bytes(r3.at[q, 0], rs_recv.at[q, 3])
            second[q, pl.ds(bp, 8), :] = second[q, pl.ds(bp, 8), :] + r3[q, 0]
            send(second.at[q, pl.ds(bp, 8)], r4.at[q, 0, pl.ds(0, 8)], rs_send.at[q, 1], rs_recv.at[q, 5], plus)
            await_bytes(r3.at[q, 1], rs_recv.at[q, 4])
            second[q, pl.ds(bm, 8), :] = second[q, pl.ds(bm, 8), :] + r3[q, 1]
            send(second.at[q, pl.ds(bm, 8)], r4.at[q, 1, pl.ds(8, 8)], rs_send.at[q, 1], rs_recv.at[q, 5], minus)
        return carry

    lax.fori_loop(0, PARTS // 2, second_forward, 0)

    chip_rows = pl.ds(aligned(chip * 16, 16), 16)
    inner_total = columns_end(3)
    cscale[...] = inner_total * (cinv[...] * cinv[...] * cinv[...])

    def finish(j, carry):
        for kind in range(2):
            q = 2 * j + kind
            cols = pl.ds(aligned(q * CH, CH), CH)
            b = ahead[1 - kind][2]
            await_bytes(r4.at[q], rs_recv.at[q, 5])
            total = second[q, pl.ds(aligned(b * 16, 16), 16), :] + r4[q, 0] + r4[q, 1]
            value = cinv[:, cols] * total - sw[chip_rows, cols].astype(F32) * cscale[:, cols]
            gwfull[k, 0, :, cols] = value[0:8]
            gwfull[k, 1, :, cols] = value[8:16]
        return carry

    lax.fori_loop(0, PARTS // 2, finish, 0)
    send(gwfull.at[k, other], gwfull.at[k, other], gw_send.at[0], gw_recv.at[0], sibling)

    loss_ref[...] = lossrow[0, pl.ds(aligned(k * OWN, LANES), OWN)]

    await_bytes(rg.at[pl.ds(0, (NZ - 1) * ZROWS)], feat_recv.at[2])
    value = rg[...]
    high = value.astype(BF16)
    value = value - high.astype(F32)
    middle = value.astype(BF16)
    low = (value - middle.astype(F32)).astype(BF16)
    scatter = onehot_t[...]
    gp_ref[...] = (
        jnp.dot(scatter, low, preferred_element_type=F32)
        + jnp.dot(scatter, middle, preferred_element_type=F32)
        + jnp.dot(scatter, high, preferred_element_type=F32)
    )

    await_bytes(gwfull.at[other, k], gw_recv.at[0])
    for core in range(NK):
        gw_ref[:, core * COLS:(core + 1) * COLS] = gwfull[core, k]

    for side in range(2):
        await_bytes(units.at[side, k], unit_send.at[side])
    for turn in range(4):
        await_bytes(crecv.at[turn, pl.ds(1, CHIPS - 1)], col_send.at[turn])
    for turn in range(3):
        cut = pl.ds(0, ROWS if turn == 1 else 2 * ROWS)
        await_bytes(rrecv.at[turn, pl.ds(1, NZ * NK - 1), :, cut], row_send.at[turn])

    def sent(q, carry):
        await_bytes(pg.at[q, pl.ds(0, 192)], rs_send.at[q, 0])
        await_bytes(second.at[q, pl.ds(0, 48)], rs_send.at[q, 1])
        return carry

    lax.fori_loop(0, PARTS, sent, 0)
    await_bytes(fsib, feat_send.at[0])
    await_bytes(fz.at[pl.ds(1, NZ - 1)], feat_send.at[1])
    await_bytes(rg.at[pl.ds(0, (NZ - 1) * ZROWS)], feat_send.at[2])
    await_bytes(gwfull.at[k, other], gw_send.at[0])


def shards(teacher_patches, student_patches, mask_index, teacher_weight, student_weight):
    vmem = pl.BlockSpec(memory_space=pltpu.VMEM)
    hbm = pl.BlockSpec(memory_space=pl.ANY)
    scratch = [
        pltpu.VMEM((WIDTH, COLS), BF16),
        pltpu.VMEM((WIDTH, COLS), BF16),
        pltpu.VMEM((WIDTH, COLS), BF16),
        pltpu.VMEM((WIDTH, COLS), BF16),
        pltpu.VMEM((1, COLS), F32),
        pltpu.VMEM((2, NK, OWN, WIDTH), F32),
        pltpu.VMEM((ROWS, WIDTH), BF16),
        pltpu.VMEM((ROWS, WIDTH), BF16),
        pltpu.VMEM((2, WIDTH, ROWS), BF16),
        pltpu.VMEM((PATCH, OWN), BF16),
        pltpu.VMEM((OWN, WIDTH), F32),
        pltpu.VMEM((OWN, LANES), F32),
        pltpu.VMEM((ROWS, COLS), F32),
        pltpu.VMEM((ROWS, COLS), F32),
        pltpu.VMEM((ROWS, LANES), F32),
        pltpu.VMEM((ROWS, LANES), F32),
        pltpu.VMEM((4, 1, COLS), F32),
        pltpu.VMEM((4, CHIPS, 1, COLS), F32),
        pltpu.VMEM((1, COLS), F32),
        pltpu.VMEM((3, 1, 2 * ROWS), F32),
        pltpu.VMEM((3, NZ * NK, 1, 2 * ROWS), F32),
        pltpu.VMEM((ROWS, LANES), F32),
        pltpu.VMEM((ROWS, LANES), F32),
        pltpu.VMEM((ROWS, CH), BF16),
        pltpu.VMEM((PARTS, WIDTH, CH), F32),
        pltpu.VMEM((PARTS, 2, 32, CH), F32),
        pltpu.VMEM((PARTS, 2, 64, CH), F32),
        pltpu.VMEM((PARTS, 2, 8, CH), F32),
        pltpu.VMEM((PARTS, 2, 16, CH), F32),
        pltpu.VMEM((PARTS, 64, CH), F32),
        pltpu.VMEM((ROWS, WIDTH), F32),
        pltpu.VMEM((OWN, WIDTH), F32),
        pltpu.VMEM((NZ, ZROWS, WIDTH), F32),
        pltpu.VMEM((OWN, WIDTH), F32),
        pltpu.VMEM((NK, NK, 8, COLS), F32),
        pltpu.VMEM((1, ROWS), F32),
        pltpu.SemaphoreType.DMA((2,)),
        pltpu.SemaphoreType.DMA((2,)),
        pltpu.SemaphoreType.DMA((2,)),
        pltpu.SemaphoreType.DMA((4,)),
        pltpu.SemaphoreType.DMA((4,)),
        pltpu.SemaphoreType.DMA((3,)),
        pltpu.SemaphoreType.DMA((3,)),
        pltpu.SemaphoreType.DMA((PARTS, 2)),
        pltpu.SemaphoreType.DMA((PARTS, 6)),
        pltpu.SemaphoreType.DMA((3,)),
        pltpu.SemaphoreType.DMA((3,)),
        pltpu.SemaphoreType.DMA((1,)),
        pltpu.SemaphoreType.DMA((1,)),
    ]
    loss, grad_weight, grad_patches = pl.pallas_call(
        kernel,
        out_shape=(
            jax.ShapeDtypeStruct((OWN,), F32),
            jax.ShapeDtypeStruct((WIDTH // DP, NK * COLS), F32),
            jax.ShapeDtypeStruct((PATCH, WIDTH), F32),
        ),
        in_specs=[vmem, vmem, vmem, hbm, hbm],
        out_specs=(vmem, vmem, vmem),
        scratch_shapes=scratch,
        compiler_params=pltpu.CompilerParams(
            collective_id=0, has_side_effects=True, vmem_limit_bytes=60 * 1024 * 1024
        ),
    )(teacher_patches, student_patches, mask_index, teacher_weight, student_weight)
    return loss, grad_weight, grad_patches


def solution(mesh):
    placed = (P("dp", None), P("dp", None), P("dp"), P(None, "proto"), P(None, "proto"))
    return jax.shard_map(
        shards,
        mesh=mesh,
        in_specs=placed,
        out_specs=(P("dp"), P("dp", "proto"), P("dp", None)),
        check_vma=False,
    )
```

time: 786 us -> 107 us (0.14); the launches traced: 774 us -> 106 us
  blocking collectives: 551 us -> 0 us
  Pallas kernels: 0 us -> 100 us
  matrix products: 88.5 us -> 0 us
  waiting for transfers between devices: 78.4 us -> 0 us
  other arithmetic: 27.6 us -> 0 us
  between operations: 15.9 us -> 0.64 us
    psum x8 -> x0, blocking collectives: 551 us -> none  [the longest x3 379 us: shards(): col_sum = col_scale * lax.psum(col_part, 'dp')]
    pallas_call x0 -> x1, Pallas kernels: none -> 100 us  [shards(): pl.pallas_call(kernel, out_shape=(jax.ShapeDtypeStruct((OWN,), F32), jax....]
    dot_general x11 -> x0, matrix products: 88.5 us -> none  [the longest x3 39.9 us: shards(): row_part = jnp.dot(teacher_exp, col_scale, precision=lax.Precision.HIGHEST)]
    psum x1 -> x0, waiting for transfers between devices: 44 us -> none  [shards(): feature_grad = lax.psum(feature_part, 'proto')]
    reduce_scatter x1 -> x0, waiting for transfers between devices: 34.4 us -> none  [shards(): lax.psum_scatter(lax.dot_general(student_unit, grad_logits, (((0,), (0,))...]
    convert_element_type x2 -> x0, other arithmetic: 17.2 us -> none  [the longest x1 10.8 us: shards(): ((probs - targets) / (rows_total * STUDENT_TEMP)).astype(jnp.bfloat16)]
  transfers between devices with their start and end apart: 2 -> 0, of which waited for: 2 -> 0; matrix products, arithmetic and copies ran while one was open for 3% -> 0% of each run, Pallas kernels for 0% -> 0%
where the time goes in v1:
time: 107 us; the launch traced here: 106 us
  Pallas kernels  100 us (93%)
  local copies, waits for them, and re-layouts  4.99 us (5%)
    pallas_call x1, Pallas kernels, shards(): pl.pallas_call(kernel, out_shape=(jax.ShapeDtypeStruct((OWN,), F32), jax....  100 us
    unnamed x3, local copies, waits for them, and re-layouts  4.99 us

profile of v1, /device:TPU:1, one launch (start us, length us, event | category | flops | bytes accessed | tf_op | source)
XLA Modules:
  0.0 105.6 jit_solution(4211391243596257001)
XLA Ops:
  0.6 100.0 %shard_map.76 = (f32[384]{0:T(512)}, f32[8,8192]{1,0:T(8,128)}, f32[768,256]{1,0:T(8,128)}) custom-call(bf16[768,256]{1,0:T(8,128)(2,1)} %tpat.1, bf16[768,256]{1,0:T(8,128)(2,1)} %spat.1, s32[384]{0:T(512)} %midx.1, bf16[256,8192]{1,0:T(8,128)(2,1)} %tw_hbm.1, bf16[256,8192]{1,0:T(8,128)(2,1)} %sw_hbm.1), custom_call_target="tpu_custom_call" | custom-call | tf_op jit(solution)/shard_map/pallas_call | solution.py:515
  100.7 1.3 %copy.11 = f32[384]{0:T(512)} copy(f32[384]{0:T(512)} %get-tuple-element.6) | data formatting | bytes 3072
  101.9 1.7 %copy.12 = f32[8,8192]{1,0:T(8,128)} copy(f32[8,8192]{1,0:T(8,128)} %get-tuple-element.7) | data formatting | bytes 524288
  103.6 2.1 %copy.13 = f32[768,256]{1,0:T(8,128)} copy(f32[768,256]{1,0:T(8,128)} %get-tuple-element.8) | data formatting | bytes 1572864

commit v2 on v0

v2 whole, which is shorter than its diff:
```python
import math

import jax
import jax.numpy as jnp
from jax import lax
from jax.experimental import pallas as pl
from jax.experimental.pallas import tpu as pltpu
from jax.sharding import PartitionSpec as P

MESH = pl.DeviceIdType.MESH
F32 = jnp.float32
BF16 = jnp.bfloat16

EPS = 1e-06
TEACHER_TEMP = 0.07
STUDENT_TEMP = 0.1
LOG2E = 1.0 / math.log(2.0)

NY, NX, NK, NZ = 4, 4, 2, 8
DP = NY * NX * NK
CHIPS = NY * NX
OWN = 384
ROWS = NK * OWN
WIDTH = 256
PATCH = 768
COLS = 4096
LANES = 128
CH = 512
PARTS = COLS // CH
TOTAL_ROWS = OWN * DP
TOTAL_PROTOS = COLS * NK * NZ
ZROWS = OWN // NZ
GRAD_SCALE = 1.0 / (TOTAL_ROWS * STUDENT_TEMP)
COL_PEERS = [(dy, dx) for dy in range(NY) for dx in range(NX)]
ROW_PEERS = [(dz, dk) for dz in range(NZ) for dk in range(NK)]
PAIRS = PARTS // 2
TILES = COLS // LANES
HALF = TILES // 2
RB = 128
STEP = 64
ZHALF = ZROWS // 2
LAG = 2
EARLY = PAIRS // 2
DELAY = 2


def farthest_first(peers, sizes):
    return sorted(peers, key=lambda at: -sum(min(d, n - d) for d, n in zip(at, sizes)))


def aligned(value, unit):
    return pl.multiple_of(value, unit)


def kernel(
    tpat_hbm, spat_hbm, midx, tw_hbm, sw_hbm,
    loss_ref, gw_ref, rg_ref,
    tpat, spat, tw, sw, tp, sp, cinv, units, tu, su, sut, srow, rinv,
    e_ref, l_ref, part, part2, csend, crecv, cscale, rsend, rrecv, rcol, ltot,
    grad, pg, r1, r2, r3, r4, second, feat, fsib, fz, rg, gwfull, lossrow,
    ipart, irecv, inner_all,
    load_sem, unit_send, unit_recv, col_send, col_recv, row_send, row_recv,
    rs_send, rs_recv, feat_send, feat_recv, gw_send, gw_recv, inner_send, inner_recv,
):
    dp = lax.axis_index("dp")
    z = lax.axis_index("proto")
    k = lax.rem(dp, NK)
    chip = lax.div(dp, NK)
    x = lax.rem(chip, NX)
    y = lax.div(chip, NX)
    other = lax.rem(k + 1, NK)

    def device(yy, xx, kk, zz):
        return ((yy * NX + xx) * NK + kk, zz)

    def chip_at(dy, dx):
        return device(lax.rem(y + dy, NY), lax.rem(x + dx, NX), k, z)

    def row_at(dz, dk):
        return device(y, x, lax.rem(k + dk, NK), lax.rem(z + dz, NZ))

    sibling = row_at(0, 1)

    def send(src, dst, send_sem, recv_sem, where):
        copy = pltpu.make_async_remote_copy(
            src_ref=src, dst_ref=dst, send_sem=send_sem, recv_sem=recv_sem,
            device_id=where, device_id_type=MESH,
        )
        copy.start()

    def await_bytes(ref, sem):
        pltpu.make_async_copy(ref, ref, sem).wait()

    leaving = []

    loads = []
    mine = pl.ds(aligned(k * COLS, COLS), COLS)
    for turn, (src, dst) in enumerate(
        ((tpat_hbm, tpat), (tw_hbm.at[:, mine], tw), (spat_hbm, spat), (sw_hbm.at[:, mine], sw))
    ):
        loads.append(pltpu.make_async_copy(src, dst, load_sem.at[turn]))
        loads[-1].start()

    barrier = pltpu.get_barrier_semaphore()
    for dz, dk in farthest_first(ROW_PEERS[1:], (NZ, NK)):
        pl.semaphore_signal(barrier, inc=1, device_id=row_at(dz, dk), device_id_type=MESH)
    for dy, dx in farthest_first(COL_PEERS[1:], (NY, NX)):
        pl.semaphore_signal(barrier, inc=1, device_id=chip_at(dy, dx), device_id_type=MESH)

    def half_rows(core):
        return pl.ds(aligned(core * OWN, LANES), OWN)

    index = midx[...].reshape(1, OWN)
    index_col = jnp.transpose(jnp.broadcast_to(index.astype(F32), (LANES, OWN)))
    lane = lax.broadcasted_iota(jnp.int32, (OWN, LANES), 1).astype(F32)
    onehot = jnp.concatenate(
        [jnp.where(index_col == lane + float(t * LANES), 1.0, 0.0) for t in range(PATCH // LANES)], axis=1
    ).astype(BF16)

    def unit_rows(side, patches, ref):
        rows = jnp.dot(onehot, patches[...], preferred_element_type=F32)
        inverse = lax.rsqrt(jnp.sum(rows * rows, axis=1, keepdims=True) + EPS)
        unit = (rows * inverse).astype(BF16)
        ref[half_rows(k), :] = unit
        units[side, k] = unit.astype(F32)
        return rows, inverse

    loads[0].wait()
    unit_rows(0, tpat, tu)
    loads[2].wait()
    srow_value, sinv = unit_rows(1, spat, su)
    srow[...] = srow_value
    rinv[...] = jnp.broadcast_to(sinv, (OWN, LANES))

    def teacher_columns(j, carry):
        cols = pl.ds(aligned(j * CH, CH), CH)
        wide = tw[:, cols].astype(F32)
        inverse = lax.rsqrt(jnp.sum(wide * wide, axis=0, keepdims=True) + EPS)
        tp[:, cols] = (wide * inverse).astype(BF16)
        return carry

    def student_columns(j, carry):
        cols = pl.ds(aligned(j * CH, CH), CH)
        wide = sw[:, cols].astype(F32)
        inverse = lax.rsqrt(jnp.sum(wide * wide, axis=0, keepdims=True) + EPS)
        for t in range(CH // LANES):
            cinv[pl.ds(j * (CH // LANES) + t, 1), :] = inverse[:, t * LANES:(t + 1) * LANES]
        sp[:, cols] = (wide * inverse).astype(BF16)
        return carry

    def teacher_exp(core, first, last, add):
        def body(j, carry):
            cols = pl.ds(aligned(j * CH, CH), CH)
            total = jnp.zeros((1, CH), F32)
            for rb in range(OWN // RB):
                at = pl.ds(aligned(core * OWN + rb * RB, RB), RB)
                value = jnp.exp2(
                    jnp.dot(tu[at, :], tp[:, cols], preferred_element_type=F32) * (LOG2E / TEACHER_TEMP)
                )
                e_ref[at, cols] = value
                total = total + jnp.sum(value, axis=0, keepdims=True)
            for t in range(CH // LANES):
                row = pl.ds(j * (CH // LANES) + t, 1)
                piece = total[:, t * LANES:(t + 1) * LANES]
                csend[0, row, :] = csend[0, row, :] + piece if add else piece
            return carry

        lax.fori_loop(first, last, body, 0)

    def student_logits(core):
        def body(j, carry):
            cols = pl.ds(aligned(j * CH, CH), CH)
            for rb in range(OWN // RB):
                at = pl.ds(aligned(core * OWN + rb * RB, RB), RB)
                value = jnp.dot(su[at, :], sp[:, cols], preferred_element_type=F32) * (LOG2E / STUDENT_TEMP)
                l_ref[at, cols] = value
                power = jnp.exp2(value)
                total = part2[at, :]
                for t in range(CH // LANES):
                    total = total + power[:, t * LANES:(t + 1) * LANES]
                part2[at, :] = total
            return carry

        lax.fori_loop(0, PARTS, body, 0)

    def columns_start(turn, half):
        cut = pl.ds(half * HALF, HALF)
        for slot, (dy, dx) in enumerate(COL_PEERS):
            if slot:
                send(
                    csend.at[turn, cut], crecv.at[turn, slot, cut],
                    col_send.at[turn, half], col_recv.at[turn, half], chip_at(dy, dx),
                )
        leaving.append((crecv.at[turn, pl.ds(1, CHIPS - 1), cut], col_send.at[turn, half]))

    def columns_end(turn, half):
        cut = pl.ds(half * HALF, HALF)
        await_bytes(crecv.at[turn, pl.ds(1, CHIPS - 1), cut], col_recv.at[turn, half])
        total = csend[turn, cut, :]
        for slot in range(1, CHIPS):
            total = total + crecv[turn, slot, cut, :]
        cscale[cut, :] = 1.0 / (total * TOTAL_PROTOS)

    def rows_start(turn, depth):
        cut = pl.ds(0, depth)
        for slot, (dz, dk) in enumerate(ROW_PEERS):
            if slot:
                send(
                    rsend.at[turn, cut], rrecv.at[turn, slot, cut],
                    row_send.at[turn], row_recv.at[turn], row_at(dz, dk),
                )
        leaving.append((rrecv.at[turn, pl.ds(1, NZ * NK - 1), cut], row_send.at[turn]))

    def rows_end(turn, depth):
        cut = pl.ds(0, depth)
        await_bytes(rrecv.at[turn, pl.ds(1, NZ * NK - 1), cut], row_recv.at[turn])
        total = rsend[turn, cut, :]
        for slot in range(1, NZ * NK):
            total = total + rrecv[turn, slot, cut, :]
        return total

    def to_column(ref, rows):
        for b in range(ROWS // LANES):
            ref[b * LANES:(b + 1) * LANES, :] = jnp.transpose(jnp.broadcast_to(rows[b:b + 1, :], (LANES, LANES)))

    def lane_sums(turn, base, ref):
        for b in range(ROWS // LANES):
            rsend[turn, base + b:base + b + 1, :] = jnp.sum(
                jnp.transpose(ref[b * LANES:(b + 1) * LANES, :]), axis=0, keepdims=True
            )

    def row_pass(half, with_loss):
        def body(rb, carry):
            at = pl.ds(aligned(rb * STEP, STEP), STEP)
            total = part[at, :] if half else jnp.zeros((STEP, LANES), F32)
            if with_loss:
                cross = part2[at, :] if half else jnp.zeros((STEP, LANES), F32)
            for t in range(half * HALF, (half + 1) * HALF):
                cut = slice(t * LANES, (t + 1) * LANES)
                value = e_ref[at, cut] * cscale[t:t + 1, :]
                total = total + value
                if with_loss:
                    cross = cross + value * l_ref[at, cut]
            part[at, :] = total
            if with_loss:
                part2[at, :] = cross
            return carry

        lax.fori_loop(0, ROWS // STEP, body, 0)

    def col_pass(turn, half):
        def body(rb, totals):
            at = pl.ds(aligned(rb * STEP, STEP), STEP)
            scale = rcol[at, :]
            out = []
            for t in range(HALF):
                cut = slice((half * HALF + t) * LANES, (half * HALF + t + 1) * LANES)
                value = e_ref[at, cut] * scale
                out.append(totals[t] + jnp.sum(value.reshape(STEP // 8, 8, LANES), axis=0))
            return tuple(out)

        totals = lax.fori_loop(0, ROWS // STEP, body, tuple(jnp.zeros((8, LANES), F32) for _ in range(HALF)))
        for t in range(HALF):
            row = half * HALF + t
            csend[turn, row:row + 1, :] = jnp.sum(totals[t], axis=0, keepdims=True)

    loads[1].wait()
    lax.fori_loop(0, PARTS, teacher_columns, 0)
    teacher_exp(k, 0, PARTS, False)
    part2[...] = jnp.zeros_like(part2)
    rsend[...] = jnp.zeros_like(rsend)

    pl.semaphore_wait(barrier, CHIPS - 1 + NZ * NK - 1)
    for side in range(2):
        send(units.at[side, k], units.at[side, k], unit_send.at[side], unit_recv.at[side], sibling)
        leaving.append((units.at[side, k], unit_send.at[side]))
    loads[3].wait()
    lax.fori_loop(0, PARTS, student_columns, 0)
    await_bytes(units.at[0, other], unit_recv.at[0])
    tu[half_rows(other), :] = units[0, other].astype(BF16)
    teacher_exp(other, 0, PARTS // 2, True)
    columns_start(0, 0)
    teacher_exp(other, PARTS // 2, PARTS, True)
    columns_start(0, 1)
    await_bytes(units.at[1, other], unit_recv.at[1])
    su[half_rows(other), :] = units[1, other].astype(BF16)
    student_logits(k)
    student_logits(other)
    lane_sums(0, 8, part2)
    for core in range(NK):
        sut[1, :, core * OWN:(core + 1) * OWN] = jnp.transpose(units[1, core]).astype(BF16)
    for xx in range(NX):
        for yy in range(NY):
            to, at = (xx * NY + yy) * 16, (yy * NX + xx) * 16
            sut[0, to:to + 16, :] = sut[1, at:at + 16, :]
    for half in range(2):
        columns_end(0, half)
        row_pass(half, False)
    lane_sums(0, 0, part)
    rows_start(0, 16)
    both = rows_end(0, 16)
    to_column(rcol, 1.0 / (both[0:8] * TOTAL_ROWS))
    for half in range(2):
        col_pass(1, half)
        columns_start(1, half)
    log_total = jnp.log(both[8:16])
    to_column(ltot, (log_total - math.log(GRAD_SCALE)) * LOG2E)
    for half in range(2):
        columns_end(1, half)
        row_pass(half, False)
    lane_sums(1, 0, part)
    rows_start(1, 8)
    row_sum = rows_end(1, 8)
    to_column(rcol, 1.0 / (row_sum * TOTAL_ROWS))
    for half in range(2):
        col_pass(2, half)
        columns_start(2, half)
    for half in range(2):
        columns_end(2, half)
        row_pass(half, True)
    lane_sums(2, 0, part)
    lane_sums(2, 8, part2)
    rows_start(2, 16)
    both = rows_end(2, 16)
    row_sum = both[0:8]
    row_scale = 1.0 / (row_sum * TOTAL_ROWS)
    to_column(rcol, row_scale * (TOTAL_ROWS * GRAD_SCALE))
    target_sum = row_sum * (row_scale * TOTAL_ROWS)
    target_logits = both[8:16] * (row_scale * (TOTAL_ROWS / LOG2E))
    lossrow[...] = log_total * target_sum - target_logits

    ahead = {0: (chip_at(0, 1), chip_at(0, 3), x), 1: (chip_at(1, 0), chip_at(3, 0), y)}
    feat[...] = jnp.zeros_like(feat)

    def make_grad(j, slot):
        for rb in range(ROWS // STEP):
            at = slice(rb * STEP, (rb + 1) * STEP)
            scale = rcol[at, :]
            shift = ltot[at, :]
            for t in range(2 * CH // LANES):
                tile = j * (2 * CH // LANES) + t
                cut = pl.ds(aligned(tile * LANES, LANES), LANES)
                probs = jnp.exp2(l_ref[at, cut] - shift)
                target = e_ref[at, cut] * cscale[pl.ds(tile, 1), :] * scale
                grad[slot, at, t * LANES:(t + 1) * LANES] = (probs - target).astype(BF16)

    def products(j, slot):
        for kind in range(2):
            q = 2 * j + kind
            value = jnp.dot(sut[kind], grad[slot, :, kind * CH:(kind + 1) * CH], preferred_element_type=F32)
            pg[q] = value
            for t in range(CH // LANES):
                cut = pl.ds(aligned(q * CH + t * LANES, LANES), LANES)
                inner = jnp.zeros((16, LANES), F32)
                for yy in range(NY):
                    for xx in range(NX):
                        at = (yy * NX + xx) * 16
                        to = (xx * NY + yy) * 16 if kind == 0 else at
                        inner = inner + (
                            sw[at:at + 16, cut].astype(F32) * value[to:to + 16, t * LANES:(t + 1) * LANES]
                        )
                ipart[q * (CH // 256) + t // 2, t % 2:t % 2 + 1, :] = jnp.sum(inner, axis=0, keepdims=True)
        cols = pl.ds(aligned(j * 2 * CH, 2 * CH), 2 * CH)
        feat[...] += lax.dot_general(
            grad[slot], sp[:, cols], (((1,), (1,)), ((), ())), preferred_element_type=F32
        )

    def first_opposite(j):
        for kind in range(2):
            q = 2 * j + kind
            plus, minus, a = ahead[kind]
            opposite = lax.rem(a + 2, 4) * 64
            send(pg.at[q, pl.ds(aligned(opposite, 32), 32)], r1.at[q, 0], rs_send.at[q, 0], rs_recv.at[q, 0], plus)
            send(pg.at[q, pl.ds(aligned(opposite + 32, 32), 32)], r1.at[q, 1], rs_send.at[q, 0], rs_recv.at[q, 1], minus)

    def first_direct(j):
        for kind in range(2):
            q = 2 * j + kind
            plus, minus, a = ahead[kind]
            ap, am = lax.rem(a + 1, 4) * 64, lax.rem(a + 3, 4) * 64
            send(pg.at[q, pl.ds(aligned(ap + 32, 32), 32)], r2.at[q, 0, pl.ds(32, 32)], rs_send.at[q, 0], rs_recv.at[q, 2], plus)
            send(pg.at[q, pl.ds(aligned(am, 32), 32)], r2.at[q, 1, pl.ds(0, 32)], rs_send.at[q, 0], rs_recv.at[q, 2], minus)

    def first_forward(j, whole):
        for kind in range(2):
            q = 2 * j + kind
            plus, minus, a = ahead[kind]
            ap = aligned(lax.rem(a + 1, 4) * 64, 64)
            am = aligned(lax.rem(a + 3, 4) * 64, 64)
            low, high = pl.ds(ap, 32), pl.ds(aligned(am + 32, 32), 32)
            await_bytes(r1.at[q, 0], rs_recv.at[q, 0])
            pg[q, low, :] = pg[q, low, :] + r1[q, 0]
            if whole:
                send(pg.at[q, pl.ds(ap, 64)], r2.at[q, 0], rs_send.at[q, 0], rs_recv.at[q, 2], plus)
            else:
                send(pg.at[q, low], r2.at[q, 0, pl.ds(0, 32)], rs_send.at[q, 0], rs_recv.at[q, 2], plus)
            await_bytes(r1.at[q, 1], rs_recv.at[q, 1])
            pg[q, high, :] = pg[q, high, :] + r1[q, 1]
            if whole:
                send(pg.at[q, pl.ds(am, 64)], r2.at[q, 1], rs_send.at[q, 0], rs_recv.at[q, 2], minus)
            else:
                send(pg.at[q, high], r2.at[q, 1, pl.ds(32, 32)], rs_send.at[q, 0], rs_recv.at[q, 2], minus)

    def second_start(j):
        for kind in range(2):
            q = 2 * j + kind
            a = ahead[kind][2]
            plus, minus, b = ahead[1 - kind]
            await_bytes(r2.at[q], rs_recv.at[q, 2])
            second[q] = pg[q, pl.ds(aligned(a * 64, 64), 64), :] + r2[q, 0] + r2[q, 1]
            opposite = lax.rem(b + 2, 4) * 16
            bp, bm = lax.rem(b + 1, 4) * 16, lax.rem(b + 3, 4) * 16
            send(second.at[q, pl.ds(aligned(opposite, 8), 8)], r3.at[q, 0], rs_send.at[q, 1], rs_recv.at[q, 3], plus)
            send(second.at[q, pl.ds(aligned(opposite + 8, 8), 8)], r3.at[q, 1], rs_send.at[q, 1], rs_recv.at[q, 4], minus)
            send(second.at[q, pl.ds(aligned(bp + 8, 8), 8)], r4.at[q, 0, pl.ds(8, 8)], rs_send.at[q, 1], rs_recv.at[q, 5], plus)
            send(second.at[q, pl.ds(aligned(bm, 8), 8)], r4.at[q, 1, pl.ds(0, 8)], rs_send.at[q, 1], rs_recv.at[q, 5], minus)

    def second_forward(j):
        for kind in range(2):
            q = 2 * j + kind
            plus, minus, b = ahead[1 - kind]
            bp = aligned(lax.rem(b + 1, 4) * 16, 8)
            bm = aligned(lax.rem(b + 3, 4) * 16 + 8, 8)
            await_bytes(r3.at[q, 0], rs_recv.at[q, 3])
            second[q, pl.ds(bp, 8), :] = second[q, pl.ds(bp, 8), :] + r3[q, 0]
            send(second.at[q, pl.ds(bp, 8)], r4.at[q, 0, pl.ds(0, 8)], rs_send.at[q, 1], rs_recv.at[q, 5], plus)
            await_bytes(r3.at[q, 1], rs_recv.at[q, 4])
            second[q, pl.ds(bm, 8), :] = second[q, pl.ds(bm, 8), :] + r3[q, 1]
            send(second.at[q, pl.ds(bm, 8)], r4.at[q, 1, pl.ds(8, 8)], rs_send.at[q, 1], rs_recv.at[q, 5], minus)

    chip_rows = pl.ds(aligned(chip * 16, 16), 16)

    def finish(j):
        for kind in range(2):
            q = 2 * j + kind
            b = ahead[1 - kind][2]
            await_bytes(r4.at[q], rs_recv.at[q, 5])
            total = second[q, pl.ds(aligned(b * 16, 16), 16), :] + r4[q, 0] + r4[q, 1]
            for t in range(CH // LANES):
                tile = q * (CH // LANES) + t
                cut = slice(tile * LANES, (tile + 1) * LANES)
                inverse = cinv[tile:tile + 1, :]
                inner = inner_all[tile // 2, tile % 2:tile % 2 + 1, :] * (inverse * inverse * inverse)
                value = inverse * total[:, t * LANES:(t + 1) * LANES] - sw[chip_rows, cut].astype(F32) * inner
                gwfull[k, 0, :, cut] = value[0:8]
                gwfull[k, 1, :, cut] = value[8:16]
        cols = pl.ds(j * 2 * CH, 2 * CH)
        send(gwfull.at[k, other, :, cols], gwfull.at[k, other, :, cols], gw_send.at[j], gw_recv.at[j], sibling)
        leaving.append((gwfull.at[k, other, :, cols], gw_send.at[j]))

    def inner_start():
        for slot, (dy, dx) in enumerate(COL_PEERS):
            if slot:
                to = lax.rem(y + dy, NY) * NX + lax.rem(x + dx, NX)
                send(ipart.at[to], irecv.at[slot], inner_send.at[0], inner_recv.at[0], chip_at(dy, dx))
        leaving.append((irecv.at[pl.ds(1, CHIPS - 1)], inner_send.at[0]))

    def inner_middle():
        await_bytes(irecv.at[pl.ds(1, CHIPS - 1)], inner_recv.at[0])
        total = ipart[chip]
        for slot in range(1, CHIPS):
            total = total + irecv[slot]
        inner_all[chip] = total
        for dy, dx in COL_PEERS[1:]:
            send(inner_all.at[chip], inner_all.at[chip], inner_send.at[1], inner_recv.at[1], chip_at(dy, dx))
        leaving.append((irecv.at[pl.ds(1, CHIPS - 1)], inner_send.at[1]))

    def inner_end():
        await_bytes(irecv.at[pl.ds(1, CHIPS - 1)], inner_recv.at[1])

    def feature_sibling():
        send(feat.at[half_rows(other)], fsib, feat_send.at[0], feat_recv.at[0], sibling)
        leaving.append((fsib, feat_send.at[0]))

    def share(where, half):
        return aligned(where * ZROWS + half * ZHALF, ZHALF)

    def feature_scatter():
        await_bytes(fsib, feat_recv.at[0])
        fsib[...] = feat[half_rows(k), :] + fsib[...]
        for half in range(2):
            for dz in range(1, NZ):
                to = lax.rem(z + dz, NZ)
                send(
                    fsib.at[pl.ds(share(to, half), ZHALF)], fz.at[half, dz],
                    feat_send.at[1 + half], feat_recv.at[1 + half], row_at(dz, 0),
                )
            leaving.append((fz.at[half, pl.ds(1, NZ - 1)], feat_send.at[1 + half]))

    def feature_gather(half):
        await_bytes(fz.at[half, pl.ds(1, NZ - 1)], feat_recv.at[1 + half])
        rows = pl.ds(share(z, half), ZHALF)
        feature = fsib[rows, :]
        for dz in range(1, NZ):
            feature = feature + fz[half, dz]
        rows_wide = srow[rows, :]
        inverse = rinv[rows, 0:1]
        rg[rows, :] = inverse * feature - rows_wide * (inverse * inverse * inverse) * jnp.sum(
            rows_wide * feature, axis=1, keepdims=True
        )
        for dz in range(1, NZ):
            send(rg.at[rows], rg.at[rows], feat_send.at[3 + half], feat_recv.at[3 + half], row_at(dz, 0))
        leaving.append((fz.at[half, pl.ds(1, NZ - 1)], feat_send.at[3 + half]))

    def feature_end(half):
        await_bytes(fz.at[half, pl.ds(1, NZ - 1)], feat_recv.at[3 + half])

    make_grad(0, 0)
    products(0, 0)
    first_opposite(0)
    first_direct(0)
    make_grad(1, 1)

    def gradient(j, carry):
        slot = lax.rem(j, 2)
        products(j, slot)
        make_grad(j + 1, 1 - slot)
        first_opposite(j)

        @pl.when(j < EARLY)
        def direct():
            first_direct(j)

        @pl.when(j >= LAG)
        def forward():
            first_forward(j - LAG, False)

        return carry

    lax.fori_loop(1, PAIRS - 1, gradient, 0)
    products(PAIRS - 1, (PAIRS - 1) % 2)
    feature_sibling()
    first_opposite(PAIRS - 1)
    inner_start()
    for j in range(PAIRS - 1 - LAG, PAIRS):
        first_forward(j, j >= EARLY)
        if j == PAIRS - 1 - LAG:
            feature_scatter()
    for j in range(PAIRS):
        second_start(j)
        if j == PAIRS // 2:
            inner_middle()
        if j == PAIRS - 2:
            feature_gather(0)
        if j >= DELAY:
            second_forward(j - DELAY)
    feature_gather(1)
    inner_end()
    for j in range(PAIRS - DELAY, PAIRS):
        second_forward(j)
        finish(j - PAIRS + DELAY)
    for j in range(DELAY, PAIRS):
        finish(j)
    loss_ref[...] = jnp.where(k == 0, lossrow[0:3, :], lossrow[3:6, :])
    feature_end(0)
    feature_end(1)
    rg_ref[...] = rg[...]
    for j in range(PAIRS):
        await_bytes(gwfull.at[other, k, :, pl.ds(j * 2 * CH, 2 * CH)], gw_recv.at[j])
    for core in range(NK):
        gw_ref[core] = gwfull[core, k]

    for ref, sem in leaving:
        await_bytes(ref, sem)

    def sent(q, carry):
        await_bytes(pg.at[q, pl.ds(0, 192)], rs_send.at[q, 0])
        await_bytes(second.at[q, pl.ds(0, 48)], rs_send.at[q, 1])
        return carry

    lax.fori_loop(0, PARTS, sent, 0)


def finish_kernel(midx, loss_part, gw_part, rg, loss_ref, gw_ref, gp_ref):
    for row in range(OWN // LANES):
        loss_ref[row * LANES:(row + 1) * LANES] = loss_part[row, :]
    for core in range(NK):
        gw_ref[:, core * COLS:(core + 1) * COLS] = gw_part[core]
    index = midx[...].reshape(1, OWN)
    patch_id = lax.broadcasted_iota(jnp.int32, (PATCH, OWN), 0)
    scatter = jnp.where(patch_id == index, 1.0, 0.0).astype(BF16)
    value = rg[...]
    high = value.astype(BF16)
    value = value - high.astype(F32)
    middle = value.astype(BF16)
    low = (value - middle.astype(F32)).astype(BF16)
    gp_ref[...] = (
        jnp.dot(scatter, low, preferred_element_type=F32)
        + jnp.dot(scatter, middle, preferred_element_type=F32)
        + jnp.dot(scatter, high, preferred_element_type=F32)
    )


def shards(teacher_patches, student_patches, mask_index, teacher_weight, student_weight):
    vmem = pl.BlockSpec(memory_space=pltpu.VMEM)
    hbm = pl.BlockSpec(memory_space=pl.ANY)
    dma = pltpu.SemaphoreType.DMA
    scratch = [
        pltpu.VMEM((PATCH, WIDTH), BF16),
        pltpu.VMEM((PATCH, WIDTH), BF16),
        pltpu.VMEM((WIDTH, COLS), BF16),
        pltpu.VMEM((WIDTH, COLS), BF16),
        pltpu.VMEM((WIDTH, COLS), BF16),
        pltpu.VMEM((WIDTH, COLS), BF16),
        pltpu.VMEM((TILES, LANES), F32),
        pltpu.VMEM((2, NK, OWN, WIDTH), F32),
        pltpu.VMEM((ROWS, WIDTH), BF16),
        pltpu.VMEM((ROWS, WIDTH), BF16),
        pltpu.VMEM((2, WIDTH, ROWS), BF16),
        pltpu.VMEM((OWN, WIDTH), F32),
        pltpu.VMEM((OWN, LANES), F32),
        pltpu.VMEM((ROWS, COLS), F32),
        pltpu.VMEM((ROWS, COLS), F32),
        pltpu.VMEM((ROWS, LANES), F32),
        pltpu.VMEM((ROWS, LANES), F32),
        pltpu.VMEM((3, TILES, LANES), F32),
        pltpu.VMEM((3, CHIPS, TILES, LANES), F32),
        pltpu.VMEM((TILES, LANES), F32),
        pltpu.VMEM((3, 16, LANES), F32),
        pltpu.VMEM((3, NZ * NK, 16, LANES), F32),
        pltpu.VMEM((ROWS, LANES), F32),
        pltpu.VMEM((ROWS, LANES), F32),
        pltpu.VMEM((2, ROWS, 2 * CH), BF16),
        pltpu.VMEM((PARTS, WIDTH, CH), F32),
        pltpu.VMEM((PARTS, 2, 32, CH), F32),
        pltpu.VMEM((PARTS, 2, 64, CH), F32),
        pltpu.VMEM((PARTS, 2, 8, CH), F32),
        pltpu.VMEM((PARTS, 2, 16, CH), F32),
        pltpu.VMEM((PARTS, 64, CH), F32),
        pltpu.VMEM((ROWS, WIDTH), F32),
        pltpu.VMEM((OWN, WIDTH), F32),
        pltpu.VMEM((2, NZ, ZHALF, WIDTH), F32),
        pltpu.VMEM((OWN, WIDTH), F32),
        pltpu.VMEM((NK, NK, 8, COLS), F32),
        pltpu.VMEM((8, LANES), F32),
        pltpu.VMEM((CHIPS, 2, LANES), F32),
        pltpu.VMEM((CHIPS, 2, LANES), F32),
        pltpu.VMEM((CHIPS, 2, LANES), F32),
        dma((4,)),
        dma((2,)),
        dma((2,)),
        dma((3, 2)),
        dma((3, 2)),
        dma((3,)),
        dma((3,)),
        dma((PARTS, 2)),
        dma((PARTS, 6)),
        dma((5,)),
        dma((5,)),
        dma((PAIRS,)),
        dma((PAIRS,)),
        dma((2,)),
        dma((2,)),
    ]
    loss_part, gw_part, row_grad = pl.pallas_call(
        kernel,
        out_shape=(
            jax.ShapeDtypeStruct((OWN // LANES, LANES), F32),
            jax.ShapeDtypeStruct((NK, WIDTH // DP, COLS), F32),
            jax.ShapeDtypeStruct((OWN, WIDTH), F32),
        ),
        in_specs=[hbm, hbm, vmem, hbm, hbm],
        out_specs=(vmem, vmem, vmem),
        scratch_shapes=scratch,
        compiler_params=pltpu.CompilerParams(
            collective_id=0, has_side_effects=True, vmem_limit_bytes=60 * 1024 * 1024
        ),
    )(teacher_patches, student_patches, mask_index, teacher_weight, student_weight)
    return pl.pallas_call(
        finish_kernel,
        out_shape=(
            jax.ShapeDtypeStruct((OWN,), F32),
            jax.ShapeDtypeStruct((WIDTH // DP, NK * COLS), F32),
            jax.ShapeDtypeStruct((PATCH, WIDTH), F32),
        ),
        in_specs=[vmem] * 4,
        out_specs=(vmem, vmem, vmem),
    )(mask_index, loss_part, gw_part, row_grad)


def solution(mesh):
    placed = (P("dp", None), P("dp", None), P("dp"), P(None, "proto"), P(None, "proto"))
    return jax.shard_map(
        shards,
        mesh=mesh,
        in_specs=placed,
        out_specs=(P("dp"), P("dp", "proto"), P("dp", None)),
        check_vma=False,
    )
```

time: 786 us -> 94.3 us (0.12); the launches traced: 774 us -> 94.2 us
  blocking collectives: 551 us -> 0 us
  Pallas kernels: 0 us -> 93.6 us
  matrix products: 88.5 us -> 0 us
  waiting for transfers between devices: 78.4 us -> 0 us
  other arithmetic: 27.6 us -> 0 us
  between operations: 15.9 us -> 0.64 us
  local copies, waits for them, and re-layouts: 12 us -> 0 us
    psum x8 -> x0, blocking collectives: 551 us -> none  [the longest x3 379 us: shards(): col_sum = col_scale * lax.psum(col_part, 'dp')]
    pallas_call x0 -> x2, Pallas kernels: none -> 93.6 us  [the longest x1 90.8 us: shards(): pl.pallas_call(kernel, out_shape=(jax.ShapeDtypeStruct((OWN // LANES, LAN...]
    dot_general x11 -> x0, matrix products: 88.5 us -> none  [the longest x3 39.9 us: shards(): row_part = jnp.dot(teacher_exp, col_scale, precision=lax.Precision.HIGHEST)]
    psum x1 -> x0, waiting for transfers between devices: 44 us -> none  [shards(): feature_grad = lax.psum(feature_part, 'proto')]
    reduce_scatter x1 -> x0, waiting for transfers between devices: 34.4 us -> none  [shards(): lax.psum_scatter(lax.dot_general(student_unit, grad_logits, (((0,), (0,))...]
    convert_element_type x2 -> x0, other arithmetic: 17.2 us -> none  [the longest x1 10.8 us: shards(): ((probs - targets) / (rows_total * STUDENT_TEMP)).astype(jnp.bfloat16)]
  transfers between devices with their start and end apart: 2 -> 0, of which waited for: 2 -> 0; matrix products, arithmetic and copies ran while one was open for 3% -> 0% of each run, Pallas kernels for 0% -> 0%
where the time goes in v2:
time: 94.3 us; the launch traced here: 94.2 us
  Pallas kernels  93.6 us (99%)
    pallas_call x1, Pallas kernels, shards(): pl.pallas_call(kernel, out_shape=(jax.ShapeDtypeStruct((OWN // LANES, LAN...  90.8 us
    pallas_call x1, Pallas kernels, shards(): pl.pallas_call(finish_kernel, out_shape=(jax.ShapeDtypeStruct((OWN,), F32...  2.8 us

profile of v2, /device:TPU:1, one launch (start us, length us, event | category | flops | bytes accessed | tf_op | source)
XLA Modules:
  0.0 94.2 jit_solution(11766319462532806115)
XLA Ops:
  0.6 90.8 %shard_map.76 = (f32[3,128]{1,0:T(4,128)}, f32[2,8,4096]{2,1,0:T(8,128)}, f32[384,256]{1,0:T(8,128)}) custom-call(bf16[768,256]{1,0:T(8,128)(2,1)} %tpat_hbm.1, bf16[768,256]{1,0:T(8,128)(2,1)} %spat_hbm.1, s32[384]{0:T(512)} %midx.3, bf16[256,8192]{1,0:T(8,128)(2,1)} %tw_hbm.1, bf16[256,8192]{1,0:T(8,128)(2,1)} %sw_hbm.1), custom_call_target="tpu_custom_call" | custom-call | tf_op jit(solution)/shard_map/pallas_call | solution.py:655
  91.4 2.8 %shard_map.77 = (f32[384]{0:T(512)}, f32[8,8192]{1,0:T(8,128)}, f32[768,256]{1,0:T(8,128)}) custom-call(s32[384]{0:T(512)} %midx.3, f32[3,128]{1,0:T(4,128)} %get-tuple-element.6.loss_part, f32[2,8,4096]{2,1,0:T(8,128)} %get-tuple-element.7.gw_part, f32[384,256]{1,0:T(8,128)} %get-tuple-element.8.rg), custom_call_target="tpu_custom_call" | custom-call | tf_op jit(solution)/shard_map/pallas_call | solution.py:669

commit v3 on v2

--- a/solution.py
+++ b/solution.py
@@ -35,17 +35,22 @@
 ROW_PEERS = [(dz, dk) for dz in range(NZ) for dk in range(NK)]
 PAIRS = PARTS // 2
 TILES = COLS // LANES
-HALF = TILES // 2
+SPLIT = 2
+PIECE = TILES // SPLIT
 RB = 128
 STEP = 64
 ZHALF = ZROWS // 2
 LAG = 2
 EARLY = PAIRS // 2
-DELAY = 2
 
 
 def farthest_first(peers, sizes):
-    return sorted(peers, key=lambda at: -sum(min(d, n - d) for d, n in zip(at, sizes)))
+    return sorted(enumerate(peers), key=lambda at: -sum(min(d, n - d) for d, n in zip(at[1], sizes)))[:-1]
+
+
+COL_ORDER = farthest_first(COL_PEERS, (NY, NX))
+ROW_ORDER = farthest_first(ROW_PEERS, (NZ, NK))
+Z_ORDER = [4, 3, 5, 2, 6, 1, 7]
 
 
 def aligned(value, unit):
@@ -57,8 +62,8 @@
     loss_ref, gw_ref, rg_ref,
     tpat, spat, tw, sw, tp, sp, cinv, units, tu, su, sut, srow, rinv,
     e_ref, l_ref, part, part2, csend, crecv, cscale, rsend, rrecv, rcol, ltot,
-    grad, pg, r1, r2, r3, r4, second, feat, fsib, fz, rg, gwfull, lossrow,
-    ipart, irecv, inner_all,
+    grad, pg, r1, r2, r4, second, feat, fsib, fz, rg, gwfull, lossrow,
+    isend, irecv,
     load_sem, unit_send, unit_recv, col_send, col_recv, row_send, row_recv,
     rs_send, rs_recv, feat_send, feat_recv, gw_send, gw_recv, inner_send, inner_recv,
 ):
@@ -102,9 +107,9 @@
         loads[-1].start()
 
     barrier = pltpu.get_barrier_semaphore()
-    for dz, dk in farthest_first(ROW_PEERS[1:], (NZ, NK)):
+    for _, (dz, dk) in ROW_ORDER:
         pl.semaphore_signal(barrier, inc=1, device_id=row_at(dz, dk), device_id_type=MESH)
-    for dy, dx in farthest_first(COL_PEERS[1:], (NY, NX)):
+    for _, (dy, dx) in COL_ORDER:
         pl.semaphore_signal(barrier, inc=1, device_id=chip_at(dy, dx), device_id_type=MESH)
 
     def half_rows(core):
@@ -183,85 +188,83 @@
 
         lax.fori_loop(0, PARTS, body, 0)
 
-    def columns_start(turn, half):
-        cut = pl.ds(half * HALF, HALF)
-        for slot, (dy, dx) in enumerate(COL_PEERS):
-            if slot:
-                send(
-                    csend.at[turn, cut], crecv.at[turn, slot, cut],
-                    col_send.at[turn, half], col_recv.at[turn, half], chip_at(dy, dx),
-                )
-        leaving.append((crecv.at[turn, pl.ds(1, CHIPS - 1), cut], col_send.at[turn, half]))
-
-    def columns_end(turn, half):
-        cut = pl.ds(half * HALF, HALF)
-        await_bytes(crecv.at[turn, pl.ds(1, CHIPS - 1), cut], col_recv.at[turn, half])
+    def columns_start(turn, piece):
+        cut = pl.ds(piece * PIECE, PIECE)
+        for slot, (dy, dx) in COL_ORDER:
+            send(
+                csend.at[turn, cut], crecv.at[turn, slot, cut],
+                col_send.at[turn, piece], col_recv.at[turn, piece], chip_at(dy, dx),
+            )
+        leaving.append((crecv.at[turn, pl.ds(1, CHIPS - 1), cut], col_send.at[turn, piece]))
+
+    def columns_end(turn, piece):
+        cut = pl.ds(piece * PIECE, PIECE)
+        await_bytes(crecv.at[turn, pl.ds(1, CHIPS - 1), cut], col_recv.at[turn, piece])
         total = csend[turn, cut, :]
         for slot in range(1, CHIPS):
             total = total + crecv[turn, slot, cut, :]
         cscale[cut, :] = 1.0 / (total * TOTAL_PROTOS)
 
-    def rows_start(turn, depth):
-        cut = pl.ds(0, depth)
-        for slot, (dz, dk) in enumerate(ROW_PEERS):
-            if slot:
-                send(
-                    rsend.at[turn, cut], rrecv.at[turn, slot, cut],
-                    row_send.at[turn], row_recv.at[turn], row_at(dz, dk),
-                )
-        leaving.append((rrecv.at[turn, pl.ds(1, NZ * NK - 1), cut], row_send.at[turn]))
-
-    def rows_end(turn, depth):
-        cut = pl.ds(0, depth)
-        await_bytes(rrecv.at[turn, pl.ds(1, NZ * NK - 1), cut], row_recv.at[turn])
-        total = rsend[turn, cut, :]
+    def rows_start(turn):
+        for slot, (dz, dk) in ROW_ORDER:
+            send(rsend.at[turn], rrecv.at[turn, slot], row_send.at[turn], row_recv.at[turn], row_at(dz, dk))
+        leaving.append((rrecv.at[turn, pl.ds(1, NZ * NK - 1)], row_send.at[turn]))
+
+    def rows_end(turn):
+        await_bytes(rrecv.at[turn, pl.ds(1, NZ * NK - 1)], row_recv.at[turn])
+        total = rsend[turn]
         for slot in range(1, NZ * NK):
-            total = total + rrecv[turn, slot, cut, :]
+            total = total + rrecv[turn, slot]
         return total
 
     def to_column(ref, rows):
         for b in range(ROWS // LANES):
             ref[b * LANES:(b + 1) * LANES, :] = jnp.transpose(jnp.broadcast_to(rows[b:b + 1, :], (LANES, LANES)))
 
-    def lane_sums(turn, base, ref):
+    def lane_sums(turn, ref):
         for b in range(ROWS // LANES):
-            rsend[turn, base + b:base + b + 1, :] = jnp.sum(
+            rsend[turn, b:b + 1, :] = jnp.sum(
                 jnp.transpose(ref[b * LANES:(b + 1) * LANES, :]), axis=0, keepdims=True
             )
 
-    def row_pass(half, with_loss):
+    def row_pass(piece):
         def body(rb, carry):
             at = pl.ds(aligned(rb * STEP, STEP), STEP)
-            total = part[at, :] if half else jnp.zeros((STEP, LANES), F32)
-            if with_loss:
-                cross = part2[at, :] if half else jnp.zeros((STEP, LANES), F32)
-            for t in range(half * HALF, (half + 1) * HALF):
+            total = part[at, :] if piece else jnp.zeros((STEP, LANES), F32)
+            for t in range(piece * PIECE, (piece + 1) * PIECE):
                 cut = slice(t * LANES, (t + 1) * LANES)
-                value = e_ref[at, cut] * cscale[t:t + 1, :]
-                total = total + value
-                if with_loss:
-                    cross = cross + value * l_ref[at, cut]
+                total = total + e_ref[at, cut] * cscale[t:t + 1, :]
             part[at, :] = total
-            if with_loss:
-                part2[at, :] = cross
             return carry
 
         lax.fori_loop(0, ROWS // STEP, body, 0)
 
-    def col_pass(turn, half):
+    def cross_pass():
+        def body(rb, carry):
+            at = pl.ds(aligned(rb * STEP, STEP), STEP)
+            total = jnp.zeros((STEP, LANES), F32)
+            for t in range(TILES):
+                cut = slice(t * LANES, (t + 1) * LANES)
+                total = total + e_ref[at, cut] * cscale[t:t + 1, :] * l_ref[at, cut]
+            part2[at, :] = total
+            return carry
+
+        lax.fori_loop(0, ROWS // STEP, body, 0)
+
+    def col_pass(turn, piece):
         def body(rb, totals):
             at = pl.ds(aligned(rb * STEP, STEP), STEP)
             scale = rcol[at, :]
             out = []
-            for t in range(HALF):
-                cut = slice((half * HALF + t) * LANES, (half * HALF + t + 1) * LANES)
+            for t in range(PIECE):
+                cut = slice((piece * PIECE + t) * LANES, (piece * PIECE + t + 1) * LANES)
                 value = e_ref[at, cut] * scale
                 out.append(totals[t] + jnp.sum(value.reshape(STEP // 8, 8, LANES), axis=0))
             return tuple(out)
 
-        totals = lax.fori_loop(0, ROWS // STEP, body, tuple(jnp.zeros((8, LANES), F32) for _ in range(HALF)))
-        for t in range(HALF):
-            row = half * HALF + t
+        totals = lax.fori_loop(0, ROWS // STEP, body, tuple(jnp.zeros((8, LANES), F32) for _ in range(PIECE)))
+        for t in range(PIECE):
+            row = piece * PIECE + t
             csend[turn, row:row + 1, :] = jnp.sum(totals[t], axis=0, keepdims=True)
 
     loads[1].wait()
@@ -278,58 +281,55 @@
     lax.fori_loop(0, PARTS, student_columns, 0)
     await_bytes(units.at[0, other], unit_recv.at[0])
     tu[half_rows(other), :] = units[0, other].astype(BF16)
-    teacher_exp(other, 0, PARTS // 2, True)
-    columns_start(0, 0)
-    teacher_exp(other, PARTS // 2, PARTS, True)
-    columns_start(0, 1)
+    for piece in range(SPLIT):
+        teacher_exp(other, piece * PARTS // SPLIT, (piece + 1) * PARTS // SPLIT, True)
+        columns_start(0, piece)
     await_bytes(units.at[1, other], unit_recv.at[1])
     su[half_rows(other), :] = units[1, other].astype(BF16)
     student_logits(k)
     student_logits(other)
-    lane_sums(0, 8, part2)
+    for piece in range(SPLIT):
+        columns_end(0, piece)
+        row_pass(piece)
+    lane_sums(0, part)
+    rows_start(0)
+    lane_sums(3, part2)
+    rows_start(3)
     for core in range(NK):
         sut[1, :, core * OWN:(core + 1) * OWN] = jnp.transpose(units[1, core]).astype(BF16)
     for xx in range(NX):
         for yy in range(NY):
             to, at = (xx * NY + yy) * 16, (yy * NX + xx) * 16
             sut[0, to:to + 16, :] = sut[1, at:at + 16, :]
-    for half in range(2):
-        columns_end(0, half)
-        row_pass(half, False)
-    lane_sums(0, 0, part)
-    rows_start(0, 16)
-    both = rows_end(0, 16)
-    to_column(rcol, 1.0 / (both[0:8] * TOTAL_ROWS))
-    for half in range(2):
-        col_pass(1, half)
-        columns_start(1, half)
-    log_total = jnp.log(both[8:16])
+    to_column(rcol, 1.0 / (rows_end(0) * TOTAL_ROWS))
+    for piece in range(SPLIT):
+        col_pass(1, piece)
+        columns_start(1, piece)
+    log_total = jnp.log(rows_end(3))
     to_column(ltot, (log_total - math.log(GRAD_SCALE)) * LOG2E)
-    for half in range(2):
-        columns_end(1, half)
-        row_pass(half, False)
-    lane_sums(1, 0, part)
-    rows_start(1, 8)
-    row_sum = rows_end(1, 8)
-    to_column(rcol, 1.0 / (row_sum * TOTAL_ROWS))
-    for half in range(2):
-        col_pass(2, half)
-        columns_start(2, half)
-    for half in range(2):
-        columns_end(2, half)
-        row_pass(half, True)
-    lane_sums(2, 0, part)
-    lane_sums(2, 8, part2)
-    rows_start(2, 16)
-    both = rows_end(2, 16)
-    row_sum = both[0:8]
+    for piece in range(SPLIT):
+        columns_end(1, piece)
+        row_pass(piece)
+    lane_sums(1, part)
+    rows_start(1)
+    to_column(rcol, 1.0 / (rows_end(1) * TOTAL_ROWS))
+    for piece in range(SPLIT):
+        col_pass(2, piece)
+        columns_start(2, piece)
+    for piece in range(SPLIT):
+        columns_end(2, piece)
+        row_pass(piece)
+    lane_sums(2, part)
+    rows_start(2)
+    cross_pass()
+    lane_sums(4, part2)
+    rows_start(4)
+    row_sum = rows_end(2)
     row_scale = 1.0 / (row_sum * TOTAL_ROWS)
     to_column(rcol, row_scale * (TOTAL_ROWS * GRAD_SCALE))
-    target_sum = row_sum * (row_scale * TOTAL_ROWS)
-    target_logits = both[8:16] * (row_scale * (TOTAL_ROWS / LOG2E))
-    lossrow[...] = log_total * target_sum - target_logits
 
     ahead = {0: (chip_at(0, 1), chip_at(0, 3), x), 1: (chip_at(1, 0), chip_at(3, 0), y)}
+    across = {0: chip_at(0, 2), 1: chip_at(2, 0)}
     feat[...] = jnp.zeros_like(feat)
 
     def make_grad(j, slot):
@@ -359,7 +359,7 @@
                         inner = inner + (
                             sw[at:at + 16, cut].astype(F32) * value[to:to + 16, t * LANES:(t + 1) * LANES]
                         )
-                ipart[q * (CH // 256) + t // 2, t % 2:t % 2 + 1, :] = jnp.sum(inner, axis=0, keepdims=True)
+                isend[0, pl.ds(q * (CH // LANES) + t, 1), :] = jnp.sum(inner, axis=0, keepdims=True)
         cols = pl.ds(aligned(j * 2 * CH, 2 * CH), 2 * CH)
         feat[...] += lax.dot_general(
             grad[slot], sp[:, cols], (((1,), (1,)), ((), ())), preferred_element_type=F32
@@ -408,39 +408,25 @@
             plus, minus, b = ahead[1 - kind]
             await_bytes(r2.at[q], rs_recv.at[q, 2])
             second[q] = pg[q, pl.ds(aligned(a * 64, 64), 64), :] + r2[q, 0] + r2[q, 1]
-            opposite = lax.rem(b + 2, 4) * 16
-            bp, bm = lax.rem(b + 1, 4) * 16, lax.rem(b + 3, 4) * 16
-            send(second.at[q, pl.ds(aligned(opposite, 8), 8)], r3.at[q, 0], rs_send.at[q, 1], rs_recv.at[q, 3], plus)
-            send(second.at[q, pl.ds(aligned(opposite + 8, 8), 8)], r3.at[q, 1], rs_send.at[q, 1], rs_recv.at[q, 4], minus)
-            send(second.at[q, pl.ds(aligned(bp + 8, 8), 8)], r4.at[q, 0, pl.ds(8, 8)], rs_send.at[q, 1], rs_recv.at[q, 5], plus)
-            send(second.at[q, pl.ds(aligned(bm, 8), 8)], r4.at[q, 1, pl.ds(0, 8)], rs_send.at[q, 1], rs_recv.at[q, 5], minus)
-
-    def second_forward(j):
-        for kind in range(2):
-            q = 2 * j + kind
-            plus, minus, b = ahead[1 - kind]
-            bp = aligned(lax.rem(b + 1, 4) * 16, 8)
-            bm = aligned(lax.rem(b + 3, 4) * 16 + 8, 8)
-            await_bytes(r3.at[q, 0], rs_recv.at[q, 3])
-            second[q, pl.ds(bp, 8), :] = second[q, pl.ds(bp, 8), :] + r3[q, 0]
-            send(second.at[q, pl.ds(bp, 8)], r4.at[q, 0, pl.ds(0, 8)], rs_send.at[q, 1], rs_recv.at[q, 5], plus)
-            await_bytes(r3.at[q, 1], rs_recv.at[q, 4])
-            second[q, pl.ds(bm, 8), :] = second[q, pl.ds(bm, 8), :] + r3[q, 1]
-            send(second.at[q, pl.ds(bm, 8)], r4.at[q, 1, pl.ds(8, 8)], rs_send.at[q, 1], rs_recv.at[q, 5], minus)
+            for slot, where in ((2, across[1 - kind]), (0, plus), (1, minus)):
+                block = pl.ds(aligned(lax.rem(b + (1, 3, 2)[slot], 4) * 16, 16), 16)
+                send(second.at[q, block], r4.at[q, slot], rs_send.at[q, 1], rs_recv.at[q, 3], where)
 
     chip_rows = pl.ds(aligned(chip * 16, 16), 16)
 
     def finish(j):
+        if j == 0:
+            inner_end(1)
         for kind in range(2):
             q = 2 * j + kind
             b = ahead[1 - kind][2]
-            await_bytes(r4.at[q], rs_recv.at[q, 5])
-            total = second[q, pl.ds(aligned(b * 16, 16), 16), :] + r4[q, 0] + r4[q, 1]
+            await_bytes(r4.at[q], rs_recv.at[q, 3])
+            total = second[q, pl.ds(aligned(b * 16, 16), 16), :] + r4[q, 0] + r4[q, 1] + r4[q, 2]
             for t in range(CH // LANES):
                 tile = q * (CH // LANES) + t
                 cut = slice(tile * LANES, (tile + 1) * LANES)
                 inverse = cinv[tile:tile + 1, :]
-                inner = inner_all[tile // 2, tile % 2:tile % 2 + 1, :] * (inverse * inverse * inverse)
+                inner = isend[2, tile:tile + 1, :] * (inverse * inverse * inverse)
                 value = inverse * total[:, t * LANES:(t + 1) * LANES] - sw[chip_rows, cut].astype(F32) * inner
                 gwfull[k, 0, :, cut] = value[0:8]
                 gwfull[k, 1, :, cut] = value[8:16]
@@ -448,25 +434,15 @@
         send(gwfull.at[k, other, :, cols], gwfull.at[k, other, :, cols], gw_send.at[j], gw_recv.at[j], sibling)
         leaving.append((gwfull.at[k, other, :, cols], gw_send.at[j]))
 
-    def inner_start():
-        for slot, (dy, dx) in enumerate(COL_PEERS):
-            if slot:
-                to = lax.rem(y + dy, NY) * NX + lax.rem(x + dx, NX)
-                send(ipart.at[to], irecv.at[slot], inner_send.at[0], inner_recv.at[0], chip_at(dy, dx))
-        leaving.append((irecv.at[pl.ds(1, CHIPS - 1)], inner_send.at[0]))
-
-    def inner_middle():
-        await_bytes(irecv.at[pl.ds(1, CHIPS - 1)], inner_recv.at[0])
-        total = ipart[chip]
-        for slot in range(1, CHIPS):
-            total = total + irecv[slot]
-        inner_all[chip] = total
-        for dy, dx in COL_PEERS[1:]:
-            send(inner_all.at[chip], inner_all.at[chip], inner_send.at[1], inner_recv.at[1], chip_at(dy, dx))
-        leaving.append((irecv.at[pl.ds(1, CHIPS - 1)], inner_send.at[1]))
-
-    def inner_end():
-        await_bytes(irecv.at[pl.ds(1, CHIPS - 1)], inner_recv.at[1])
+    def inner_start(turn):
+        for slot in (2, 1, 3):
+            where = chip_at(0, slot) if turn == 0 else chip_at(slot, 0)
+            send(isend.at[turn], irecv.at[turn, slot], inner_send.at[turn], inner_recv.at[turn], where)
+        leaving.append((irecv.at[turn, pl.ds(1, 3)], inner_send.at[turn]))
+
+    def inner_end(turn):
+        await_bytes(irecv.at[turn, pl.ds(1, 3)], inner_recv.at[turn])
+        isend[turn + 1] = isend[turn] + irecv[turn, 1] + irecv[turn, 2] + irecv[turn, 3]
 
     def feature_sibling():
         send(feat.at[half_rows(other)], fsib, feat_send.at[0], feat_recv.at[0], sibling)
@@ -479,7 +455,7 @@
         await_bytes(fsib, feat_recv.at[0])
         fsib[...] = feat[half_rows(k), :] + fsib[...]
         for half in range(2):
-            for dz in range(1, NZ):
+            for dz in Z_ORDER:
                 to = lax.rem(z + dz, NZ)
                 send(
                     fsib.at[pl.ds(share(to, half), ZHALF)], fz.at[half, dz],
@@ -498,7 +474,7 @@
         rg[rows, :] = inverse * feature - rows_wide * (inverse * inverse * inverse) * jnp.sum(
             rows_wide * feature, axis=1, keepdims=True
         )
-        for dz in range(1, NZ):
+        for dz in Z_ORDER:
             send(rg.at[rows], rg.at[rows], feat_send.at[3 + half], feat_recv.at[3 + half], row_at(dz, 0))
         leaving.append((fz.at[half, pl.ds(1, NZ - 1)], feat_send.at[3 + half]))
 
@@ -530,27 +506,27 @@
     lax.fori_loop(1, PAIRS - 1, gradient, 0)
     products(PAIRS - 1, (PAIRS - 1) % 2)
     feature_sibling()
+    inner_start(0)
     first_opposite(PAIRS - 1)
-    inner_start()
     for j in range(PAIRS - 1 - LAG, PAIRS):
         first_forward(j, j >= EARLY)
         if j == PAIRS - 1 - LAG:
             feature_scatter()
-    for j in range(PAIRS):
-        second_start(j)
-        if j == PAIRS // 2:
-            inner_middle()
-        if j == PAIRS - 2:
-            feature_gather(0)
-        if j >= DELAY:
-            second_forward(j - DELAY)
+    inner_end(0)
+    inner_start(1)
+    second_start(0)
+    second_start(1)
+    second_start(2)
+    feature_gather(0)
+    second_start(3)
+    finish(0)
+    finish(1)
     feature_gather(1)
-    inner_end()
-    for j in range(PAIRS - DELAY, PAIRS):
-        second_forward(j)
-        finish(j - PAIRS + DELAY)
-    for j in range(DELAY, PAIRS):
-        finish(j)
+    finish(2)
+    finish(3)
+    target_sum = row_sum * (row_scale * TOTAL_ROWS)
+    target_logits = rows_end(4) * (row_scale * (TOTAL_ROWS / LOG2E))
+    lossrow[...] = log_total * target_sum - target_logits
     loss_ref[...] = jnp.where(k == 0, lossrow[0:3, :], lossrow[3:6, :])
     feature_end(0)
     feature_end(1)
@@ -616,16 +592,15 @@
         pltpu.VMEM((3, TILES, LANES), F32),
         pltpu.VMEM((3, CHIPS, TILES, LANES), F32),
         pltpu.VMEM((TILES, LANES), F32),
-        pltpu.VMEM((3, 16, LANES), F32),
-        pltpu.VMEM((3, NZ * NK, 16, LANES), F32),
+        pltpu.VMEM((5, 8, LANES), F32),
+        pltpu.VMEM((5, NZ * NK, 8, LANES), F32),
         pltpu.VMEM((ROWS, LANES), F32),
         pltpu.VMEM((ROWS, LANES), F32),
         pltpu.VMEM((2, ROWS, 2 * CH), BF16),
         pltpu.VMEM((PARTS, WIDTH, CH), F32),
         pltpu.VMEM((PARTS, 2, 32, CH), F32),
         pltpu.VMEM((PARTS, 2, 64, CH), F32),
-        pltpu.VMEM((PARTS, 2, 8, CH), F32),
-        pltpu.VMEM((PARTS, 2, 16, CH), F32),
+        pltpu.VMEM((PARTS, 3, 16, CH), F32),
         pltpu.VMEM((PARTS, 64, CH), F32),
         pltpu.VMEM((ROWS, WIDTH), F32),
         pltpu.VMEM((OWN, WIDTH), F32),
@@ -633,18 +608,17 @@
         pltpu.VMEM((OWN, WIDTH), F32),
         pltpu.VMEM((NK, NK, 8, COLS), F32),
         pltpu.VMEM((8, LANES), F32),
-        pltpu.VMEM((CHIPS, 2, LANES), F32),
-        pltpu.VMEM((CHIPS, 2, LANES), F32),
-        pltpu.VMEM((CHIPS, 2, LANES), F32),
+        pltpu.VMEM((3, TILES, LANES), F32),
+        pltpu.VMEM((2, 4, TILES, LANES), F32),
         dma((4,)),
         dma((2,)),
         dma((2,)),
-        dma((3, 2)),
-        dma((3, 2)),
-        dma((3,)),
-        dma((3,)),
+        dma((3, SPLIT)),
+        dma((3, SPLIT)),
+        dma((5,)),
+        dma((5,)),
         dma((PARTS, 2)),
-        dma((PARTS, 6)),
+        dma((PARTS, 4)),
         dma((5,)),
         dma((5,)),
         dma((PAIRS,)),

time: 94.3 us -> 87.3 us (0.926)
  Pallas kernels: 93.6 us -> 86.1 us
    pallas_call x1, Pallas kernels: 90.8 us -> 83.3 us  [shards(): pl.pallas_call(kernel, out_shape=(jax.ShapeDtypeStruct((OWN // LANES, LAN...]
where the time goes in v3:
time: 87.3 us; the launch traced here: 86.7 us
  Pallas kernels  86.1 us (99%)
    pallas_call x1, Pallas kernels, shards(): pl.pallas_call(kernel, out_shape=(jax.ShapeDtypeStruct((OWN // LANES, LAN...  83.3 us
    pallas_call x1, Pallas kernels, shards(): pl.pallas_call(finish_kernel, out_shape=(jax.ShapeDtypeStruct((OWN,), F32...  2.8 us

profile of v3, /device:TPU:1, one launch (start us, length us, event | category | flops | bytes accessed | tf_op | source)
XLA Modules:
  0.0 86.7 jit_solution(1336729115697197982)
XLA Ops:
  0.6 83.3 %shard_map.76 = (f32[3,128]{1,0:T(4,128)}, f32[2,8,4096]{2,1,0:T(8,128)}, f32[384,256]{1,0:T(8,128)}) custom-call(bf16[768,256]{1,0:T(8,128)(2,1)} %tpat_hbm.1, bf16[768,256]{1,0:T(8,128)(2,1)} %spat_hbm.1, s32[384]{0:T(512)} %midx.3, bf16[256,8192]{1,0:T(8,128)(2,1)} %tw_hbm.1, bf16[256,8192]{1,0:T(8,128)(2,1)} %sw_hbm.1), custom_call_target="tpu_custom_call" | custom-call | tf_op jit(solution)/shard_map/pallas_call | solution.py:629
  83.9 2.8 %shard_map.77 = (f32[384]{0:T(512)}, f32[8,8192]{1,0:T(8,128)}, f32[768,256]{1,0:T(8,128)}) custom-call(s32[384]{0:T(512)} %midx.3, f32[3,128]{1,0:T(4,128)} %get-tuple-element.6.loss_part, f32[2,8,4096]{2,1,0:T(8,128)} %get-tuple-element.7.gw_part, f32[384,256]{1,0:T(8,128)} %get-tuple-element.8.rg), custom_call_target="tpu_custom_call" | custom-call | tf_op jit(solution)/shard_map/pallas_call | solution.py:643

commit v4 on v3

--- a/solution.py
+++ b/solution.py
@@ -153,11 +153,11 @@
         sp[:, cols] = (wide * inverse).astype(BF16)
         return carry
 
-    def teacher_exp(core, first, last, add):
+    def teacher_exp(core, first, last, add, blocks=range(OWN // RB)):
         def body(j, carry):
             cols = pl.ds(aligned(j * CH, CH), CH)
             total = jnp.zeros((1, CH), F32)
-            for rb in range(OWN // RB):
+            for rb in blocks:
                 at = pl.ds(aligned(core * OWN + rb * RB, RB), RB)
                 value = jnp.exp2(
                     jnp.dot(tu[at, :], tp[:, cols], preferred_element_type=F32) * (LOG2E / TEACHER_TEMP)
@@ -274,17 +274,22 @@
     rsend[...] = jnp.zeros_like(rsend)
 
     pl.semaphore_wait(barrier, CHIPS - 1 + NZ * NK - 1)
-    for side in range(2):
-        send(units.at[side, k], units.at[side, k], unit_send.at[side], unit_recv.at[side], sibling)
-        leaving.append((units.at[side, k], unit_send.at[side]))
+    blocks = [(0, rb * RB, RB) for rb in range(OWN // RB)] + [(1, 0, OWN)]
+    for turn, (side, at, depth) in enumerate(blocks):
+        piece = units.at[side, k, pl.ds(at, depth)]
+        send(piece, piece, unit_send.at[turn], unit_recv.at[turn], sibling)
+        leaving.append((piece, unit_send.at[turn]))
     loads[3].wait()
     lax.fori_loop(0, PARTS, student_columns, 0)
-    await_bytes(units.at[0, other], unit_recv.at[0])
-    tu[half_rows(other), :] = units[0, other].astype(BF16)
     for piece in range(SPLIT):
-        teacher_exp(other, piece * PARTS // SPLIT, (piece + 1) * PARTS // SPLIT, True)
+        for rb in range(OWN // RB):
+            if piece == 0:
+                rows = pl.ds(rb * RB, RB)
+                await_bytes(units.at[0, other, rows], unit_recv.at[rb])
+                tu[pl.ds(aligned(other * OWN + rb * RB, RB), RB), :] = units[0, other, rows, :].astype(BF16)
+            teacher_exp(other, piece * PARTS // SPLIT, (piece + 1) * PARTS // SPLIT, True, (rb,))
         columns_start(0, piece)
-    await_bytes(units.at[1, other], unit_recv.at[1])
+    await_bytes(units.at[1, other], unit_recv.at[OWN // RB])
     su[half_rows(other), :] = units[1, other].astype(BF16)
     student_logits(k)
     student_logits(other)
@@ -611,8 +616,8 @@
         pltpu.VMEM((3, TILES, LANES), F32),
         pltpu.VMEM((2, 4, TILES, LANES), F32),
         dma((4,)),
-        dma((2,)),
-        dma((2,)),
+        dma((4,)),
+        dma((4,)),
         dma((3, SPLIT)),
         dma((3, SPLIT)),
         dma((5,)),

time: 87.3 us -> 89.5 us (1.025)
  Pallas kernels: 86.1 us -> 87.9 us
    pallas_call x1, Pallas kernels: 83.3 us -> 85.1 us  [shards(): pl.pallas_call(kernel, out_shape=(jax.ShapeDtypeStruct((OWN // LANES, LAN...]
where the time goes in v4:
time: 89.5 us; the launch traced here: 88.6 us
  Pallas kernels  87.9 us (98%)
    pallas_call x1, Pallas kernels, shards(): pl.pallas_call(kernel, out_shape=(jax.ShapeDtypeStruct((OWN // LANES, LAN...  85.1 us
    pallas_call x1, Pallas kernels, shards(): pl.pallas_call(finish_kernel, out_shape=(jax.ShapeDtypeStruct((OWN,), F32...  2.8 us

profile of v4, /device:TPU:1, one launch (start us, length us, event | category | flops | bytes accessed | tf_op | source)
XLA Modules:
  0.0 88.6 jit_solution(15750434187028005144)
XLA Ops:
  0.6 85.1 %shard_map.76 = (f32[3,128]{1,0:T(4,128)}, f32[2,8,4096]{2,1,0:T(8,128)}, f32[384,256]{1,0:T(8,128)}) custom-call(bf16[768,256]{1,0:T(8,128)(2,1)} %tpat_hbm.1, bf16[768,256]{1,0:T(8,128)(2,1)} %spat_hbm.1, s32[384]{0:T(512)} %midx.3, bf16[256,8192]{1,0:T(8,128)(2,1)} %tw_hbm.1, bf16[256,8192]{1,0:T(8,128)(2,1)} %sw_hbm.1), custom_call_target="tpu_custom_call" | custom-call | tf_op jit(solution)/shard_map/pallas_call | solution.py:634
  85.8 2.8 %shard_map.77 = (f32[384]{0:T(512)}, f32[8,8192]{1,0:T(8,128)}, f32[768,256]{1,0:T(8,128)}) custom-call(s32[384]{0:T(512)} %midx.3, f32[3,128]{1,0:T(4,128)} %get-tuple-element.6.loss_part, f32[2,8,4096]{2,1,0:T(8,128)} %get-tuple-element.7.gw_part, f32[384,256]{1,0:T(8,128)} %get-tuple-element.8.rg), custom_call_target="tpu_custom_call" | custom-call | tf_op jit(solution)/shard_map/pallas_call | solution.py:648
